TPU v7x, 256 devices: a whole 4x4x8 slice. The times are simulated.
256 devices in a mesh: dp: 32 (over y_lo, z, core), fsdp: 8 (over x, y_hi).
Axes of the slice: x: 4, y: 4 (y_hi: 2, y_lo: 2; y = y_hi * 2 + y_lo), z: 8, core: 2. Of those that a mesh axis runs over, the one named last changes fastest.
Arguments:
- hidden_in: bfloat16 [32768, 4096], P(('dp', 'fsdp')), may hold values from -6 to 6
- lengths: int32 [32], P('dp'), may hold values from 1 to 1024, 24576 in all
- cartridge: bfloat16 [2, 512, 1024], P(None, None, 'fsdp'), may hold values from -96 to 96
- norm_gain: float32 [4096], replicated, may hold values from 0.1 to 1.9
- w_query: bfloat16 [4096, 4096], P('dp', 'fsdp'), may hold values from -0.09375 to 0.09375
- w_keyval: bfloat16 [4096, 2, 1024], P('dp', None, 'fsdp'), may hold values from -0.09375 to 0.09375
- cotangent: bfloat16 [32768, 4096], P('dp', 'fsdp'), may hold values from -6 to 6
Outputs:
- attn_heads: bfloat16 [32768, 4096], P('dp', 'fsdp')
- cart_grad: float32 [2, 512, 1024], P(None, None, 'fsdp')
Inputs may be any that keep to these rules, and one draw needn't show every extreme that they name: `lengths`: positions at or past a conversation's length are padding.
All inputs are finite; a program needn't handle non-finite values. No bound on the sum of `lengths` on one device may be relied on, other than what follows from the above.
Results may differ from a plain program's by a relative error of at most 0.0095.
The roundings to bfloat16 on the way count: a program that leaves them out, or rounds other values in their place, can miss the bound.
Values may be sent and summed in bfloat16 or wider, within the bound.
A program may use at most 64 MiB of HBM per device.

v0:
```python
import jax
import jax.numpy as jnp
from jax import lax
from jax.sharding import PartitionSpec as P

HD = 128


epsilon = 1e-05
rope_base = 500000.0


def normalize(hidden, norm_gain):
    floated = hidden.astype(jnp.float32)
    inverse = lax.rsqrt(jnp.mean(floated * floated, axis=-1, keepdims=True) + epsilon)
    return (floated * inverse * norm_gain).astype(jnp.bfloat16)


def rotate(matrix, positions, turn_sign, head_dim):
    row_count = matrix.shape[0]
    half_dim = head_dim // 2
    per_head = matrix.reshape(row_count, -1, head_dim)
    exponent = jnp.arange(half_dim).astype(jnp.float32) * (-2.0 / head_dim)
    frequency = jnp.power(jnp.float32(rope_base), exponent)
    angles = positions.astype(jnp.float32)[:, None] * frequency[None, :]
    cosine = jnp.cos(angles)[:, None, :]
    sine_part = turn_sign * jnp.sin(angles)[:, None, :]
    front_half = per_head[..., :half_dim]
    back_half = per_head[..., half_dim:]
    turned = jnp.concatenate(
        [front_half * cosine - back_half * sine_part, back_half * cosine + front_half * sine_part],
        axis=-1,
    )
    return turned.reshape(row_count, -1)


def finish(query_sum, pair_sum, positions, head_dim):
    query = rotate(query_sum, positions, 1.0, head_dim).astype(jnp.bfloat16)
    half_width = pair_sum.shape[1] // 2
    key_new = rotate(pair_sum[:, :half_width], positions, 1.0, head_dim).astype(jnp.bfloat16)
    value_new = pair_sum[:, half_width:].astype(jnp.bfloat16)
    return (query, key_new, value_new)


def block_attention(
    query_block, grad_block, key_head, value_head, row_start, length, cart_len, head_dim
):
    block = query_block.shape[0]
    key_count = key_head.shape[0]
    score_scale = head_dim ** (-0.5)
    scores = (
        lax.dot_general(
            query_block, key_head, (((1,), (1,)), ((), ())), preferred_element_type=jnp.float32
        )
        * score_scale
    )
    key_index = jnp.arange(key_count)[None, :]
    query_index = row_start + jnp.arange(block)[:, None]
    allowed = (key_index < cart_len) | (key_index - cart_len <= query_index) & (
        key_index - cart_len < length
    )
    scores = jnp.where(allowed, scores, -jnp.inf)
    row_max = jnp.max(scores, axis=-1, keepdims=True)
    exponent = jnp.exp(scores - row_max)
    attn_prob = exponent / jnp.sum(exponent, axis=-1, keepdims=True)
    prob_b = attn_prob.astype(jnp.bfloat16)
    mixed = jnp.dot(prob_b, value_head, preferred_element_type=jnp.float32).astype(jnp.bfloat16)
    d_prob = lax.dot_general(
        grad_block, value_head, (((1,), (1,)), ((), ())), preferred_element_type=jnp.float32
    )
    d_value = lax.dot_general(
        prob_b[:, :cart_len],
        grad_block,
        (((0,), (0,)), ((), ())),
        preferred_element_type=jnp.float32,
    )
    d_score = attn_prob * (d_prob - jnp.sum(attn_prob * d_prob, axis=-1, keepdims=True))
    d_score_b = d_score.astype(jnp.bfloat16)
    d_key = (
        lax.dot_general(
            d_score_b[:, :cart_len],
            query_block,
            (((0,), (0,)), ((), ())),
            preferred_element_type=jnp.float32,
        )
        * score_scale
    )
    return (mixed, d_key, d_value)


def on_device(hidden_in, lengths, cartridge, norm_gain, w_query, w_keyval, cotangent):
    head_dim = HD
    shard_rows = hidden_in.shape[0]
    tokens = shard_rows * lax.axis_size("fsdp")
    cart_len = cartridge.shape[1]
    length = lengths[0]
    query_width = w_query.shape[1]
    key_width = w_keyval.shape[2]
    normed_rows = normalize(hidden_in, norm_gain)
    query_weight, pair_weight = (
        lax.all_gather(w_query, "dp", axis=0, tiled=True),
        lax.all_gather(w_keyval, "dp", axis=0, tiled=True),
    )
    pair_flat = pair_weight.reshape(pair_weight.shape[0], -1)
    piece = lax.all_gather(normed_rows, "fsdp", axis=0, tiled=True)
    count = piece.shape[0]
    spots = cart_len + jnp.int32(0) + jnp.arange(count)
    query_sum = jnp.dot(piece, query_weight, preferred_element_type=jnp.float32)
    pair_sum = jnp.dot(piece, pair_flat, preferred_element_type=jnp.float32)
    packed = jnp.concatenate(finish(query_sum, pair_sum, spots, head_dim), axis=1)
    query = packed[:, :query_width]
    key_new = packed[:, query_width : query_width + key_width]
    value_new = packed[:, query_width + key_width :]
    key_rows = jnp.concatenate([cartridge[0], key_new], axis=0)
    value_rows = jnp.concatenate([cartridge[1], value_new], axis=0)
    live_rows = (jnp.arange(tokens) < length)[:, None]
    grad = jnp.where(live_rows, cotangent, jnp.zeros_like(cotangent))
    block = min(512, tokens)
    block_count = tokens // block
    group = query_width // key_width
    mixed_all = jnp.zeros((tokens, query_width), jnp.bfloat16)

    def step(item, state):
        mixed_state, key_total, value_total = state
        member = item // block_count
        row_start = item % block_count * block
        column = (0 + member) * head_dim
        query_block = lax.dynamic_slice(query, (row_start, column), (block, head_dim))
        grad_block = lax.dynamic_slice(grad, (row_start, column), (block, head_dim))
        mixed, d_key, d_value = block_attention(
            query_block, grad_block, key_rows, value_rows, row_start, length, cart_len, head_dim
        )
        mixed_state = lax.dynamic_update_slice(mixed_state, mixed, (row_start, column))
        return (mixed_state, key_total + d_key, value_total + d_value)

    empty = jnp.zeros((cart_len, head_dim), jnp.float32)
    mixed_all, key_total, value_total = lax.fori_loop(
        0, group * block_count, step, (mixed_all, empty, empty)
    )
    key_summed, value_summed = lax.psum((key_total, value_total), "dp")
    return (mixed_all, jnp.stack([key_summed, value_summed]))


def solution(mesh):
    in_specs = (
        P(("dp", "fsdp"), None),
        P("dp"),
        P(None, None, "fsdp"),
        P(),
        P("dp", "fsdp"),
        P("dp", None, "fsdp"),
        P("dp", "fsdp"),
    )
    out_specs = (P("dp", "fsdp"), P(None, None, "fsdp"))
    return jax.shard_map(
        on_device, mesh=mesh, in_specs=in_specs, out_specs=out_specs, check_vma=False
    )
```

profile of v0, /device:TPU:1, one launch (start us, length us, event | category | flops | bytes accessed | tf_op | source)
XLA Modules:
  0.0 598.5 jit_solution(11088660186348892804)
XLA Ops:
  9.5 2.5 fusion.16
  16.0 62.8 %all-gather.8.cloned.1.call-done = bf16[4096,2,128]{2,1,0:T(2,128)(2,1)} async-done(((bf16[128,2,128]{2,1,0:T(2,128)(2,1)}), bf16[4096,2,128]{2,1,0:T(2,128)(2,1)}) %all-gather.8.cloned.1.call-update) | async-done | bytes 2097168 | tf_op jit(solution)/shard_map/all_gather | solution.py:102
  78.8 116.1 %all-gather.4.cloned.1.call-done = bf16[1024,4096]{1,0:T(8,128)(2,1)} async-done(((bf16[128,4096]{1,0:T(8,128)(2,1)}), bf16[1024,4096]{1,0:T(8,128)(2,1)}) %all-gather.4.cloned.1.call-update) | async-done | bytes 8388624 | tf_op jit(solution)/shard_map/all_gather | solution.py:105
  194.9 6.3 %fusion.17 = f32[1024,256]{0,1:T(8,128)S(1)} fusion(bf16[1024,4096]{1,0:T(8,128)(2,1)} %all-gather.4.cloned.1.call-done, bf16[512,8,2,128]{3,2,1,0:T(2,128)(2,1)} %bitcast.36), kind=kOutput, calls=%fused_computation.30 | convolution fusion | flops 2147483648 | bytes 11534336 | tf_op jit(solution)/shard_map/dot_general | solution.py:109
  203.1 59.3 %all-gather.6.cloned.1.call-done = bf16[4096,512]{1,0:T(8,128)(2,1)} async-done(((bf16[128,512]{1,0:T(8,128)(2,1)}), bf16[4096,512]{1,0:T(8,128)(2,1)}) %all-gather.6.cloned.1.call-update) | async-done | bytes 4194320 | tf_op jit(solution)/shard_map/all_gather | solution.py:101
  262.4 8.2 %fusion.31 = f32[1024,512]{0,1:T(8,128)S(1)} fusion(bf16[1024,4096]{1,0:T(8,128)(2,1)} %all-gather.4.cloned.1.call-done, bf16[4096,512]{1,0:T(8,128)(2,1)} %all-gather.6.cloned.1.call-done), kind=kOutput, calls=%fused_computation.61 | convolution fusion | flops 4294967296 | bytes 14680064 | tf_op jit(solution)/shard_map/dot_general | solution.py:108
  272.2 95.7 %while.20 = (s32[]{:T(128)}, bf16[1024,512]{1,0:T(8,128)(2,1)}, f32[512,128]{1,0:T(8,128)}, f32[512,128]{1,0:T(8,128)}, s32[]{:T(128)}, /*index=5*/bf16[1024,512...) while((s32[]{:T(128)}, bf16[1024,512]{1,0:T(8,128)(2,1)}, ...), condition=%wide.region_5.6_spmd.clone, body=%wide.region_1.5_spmd.clone.sunk | while | flops 749605888 | bytes 39099916 | solution.py:137
  274.7 3.4 multiply_reduce_fusion.2
  278.1 2.4 fusion.62
  286.5 3.4 multiply_reduce_fusion.2
  289.9 2.5 fusion.62
  298.5 3.4 multiply_reduce_fusion.2
  301.9 2.5 fusion.62
  310.5 3.4 multiply_reduce_fusion.2
  313.9 2.5 fusion.62
  322.5 3.4 multiply_reduce_fusion.2
  325.9 2.5 fusion.62
  334.5 3.4 multiply_reduce_fusion.2
  337.9 2.5 fusion.62
  346.5 3.4 multiply_reduce_fusion.2
  349.9 2.5 fusion.62
  358.5 3.4 multiply_reduce_fusion.2
  361.9 2.5 fusion.62
  367.9 222.1 %all-reduce.3.cloned.1.call-done = (f32[1,512,128]{2,1,0:T(8,128)}, f32[1,512,128]{2,1,0:T(8,128)}) async-done(((f32[1,512,128]{2,1,0:T(8,128)}, f32[1,512,128]{2,1,0:T(8,128)}), (f32[1,512,128]{2,1,0:T(8,128)}, f32[1,512,128]{2,1,0:T(8,128)})) %all-reduce.3.cloned.1.call-update) | async-done | bytes 524304 | tf_op jit(solution)/shard_map/psum | solution.py:140
  (164 shorter events, 58.4 us)
Async XLA Ops:
  7.2 5.7 copy-start.5
  7.2 7.6 %copy-start.2 = (bf16[1024,512]{1,0:T(8,128)(2,1)S(1)}, bf16[1024,512]{1,0:T(8,128)(2,1)}, u32[]{:S(2)}) copy-start(bf16[1024,512]{1,0:T(8,128)(2,1)} %param.15) | copy-start | bytes 3145732
  7.2 71.6 %all-gather.8.cloned.1.call-start = ((), (), s32[]{:S(2)}) async-start(), calls=%async_computation.2 | async-start | bytes 2162688 | tf_op jit(solution)/shard_map/all_gather | solution.py:102
  7.9 187.0 %all-gather.4.cloned.1.call-start = ((), (), s32[]{:S(2)}) async-start(), calls=%async_computation | async-start | bytes 9437184 | tf_op jit(solution)/shard_map/all_gather | solution.py:105
  12.0 250.4 %all-gather.6.cloned.1.call-start = ((), (), s32[]{:S(2)}) async-start(), calls=%async_computation.1 | async-start | bytes 4325376 | tf_op jit(solution)/shard_map/all_gather | solution.py:101
  12.8 577.3 %all-reduce.3.cloned.1.call-start = ((), (), s32[]{:S(2)}) async-start(), calls=%async_computation.3 | async-start | bytes 1048576 | tf_op jit(solution)/shard_map/psum | solution.py:140
  280.7 3.2 copy-start.1
  280.7 3.2 copy-start.4
  283.9 2.5 copy-start.3
  292.6 3.3 copy-start.1
  292.6 3.3 copy-start.4
  295.9 2.5 copy-start.3
  304.6 3.3 copy-start.1
  304.6 3.3 copy-start.4
  316.6 3.3 copy-start.1
  316.6 3.3 copy-start.4
  328.6 3.3 copy-start.1
  328.6 3.3 copy-start.4
  340.6 3.3 copy-start.1
  340.6 3.3 copy-start.4
  352.6 3.3 copy-start.1
  352.6 3.3 copy-start.4
  364.6 3.3 copy-start.1
  364.6 3.3 copy-start.4
  (14 other events, 35.5 us)
Sparse Core Ops, SparseCore 0:
  9.9 68.8 all-gather.7
  82.0 112.8 all-gather.3
  196.8 65.5 all-gather.5
  368.1 221.9 all-reduce.2
where the time goes:
time: 599 us; the launch traced here: 598 us
  waiting for transfers between devices  462 us (77%)
  matrix products  97.9 us (16%)
  other arithmetic  21.4 us (4%)
  between operations  14.6 us (2%)
    psum x1, waiting for transfers between devices, on_device(): key_summed, value_summed = lax.psum((key_total, value_total), 'dp')  222 us
    all_gather x1, waiting for transfers between devices, on_device(): piece = lax.all_gather(normed_rows, 'fsdp', axis=0, tiled=True)  116 us
    all_gather x1, waiting for transfers between devices, on_device(): lax.all_gather(w_keyval, 'dp', axis=0, tiled=True)  62.8 us
    all_gather x1, waiting for transfers between devices, on_device(): lax.all_gather(w_query, 'dp', axis=0, tiled=True)  59.3 us
    dot_general x8, matrix products, block_attention(): lax.dot_general(grad_block, value_head, (((1,), (1,)), ((), ())), preferr...  27.4 us
    dot_general x8, matrix products, block_attention(): lax.dot_general(d_score_b[:, :cart_len], query_block, (((0,), (0,)), ((),...  19.9 us
    dot_general x8, matrix products, block_attention(): lax.dot_general(prob_b[:, :cart_len], grad_block, (((0,), (0,)), ((), ())...  16.5 us
  transfers between devices with their start and end apart: 4, of which 4 were waited for; matrix products, arithmetic and copies ran while one was open for 2% of the time, Pallas kernels for 0%

commit v1 on v0

v1 whole, which is shorter than its diff:
```python
import functools
import math

import jax
import jax.numpy as jnp
from jax import lax
from jax.experimental import pallas as pl
from jax.experimental.pallas import tpu as pltpu
from jax.sharding import PartitionSpec as P

HD = 128
MESH = pl.DeviceIdType.MESH
EPS = 1e-05
ROPE_BASE = 500000.0
F32 = jnp.float32
BF16 = jnp.bfloat16
ROWS = 256


def normalize(hidden, norm_gain):
    floated = hidden.astype(F32)
    inverse = lax.rsqrt(jnp.mean(floated * floated, axis=-1, keepdims=True) + EPS)
    return (floated * inverse * norm_gain).astype(BF16)


def rotate(matrix, positions, head_dim):
    row_count = matrix.shape[0]
    half_dim = head_dim // 2
    per_head = matrix.reshape(row_count, -1, head_dim)
    exponent = jnp.arange(half_dim).astype(F32) * (-2.0 / head_dim)
    frequency = jnp.power(jnp.float32(ROPE_BASE), exponent)
    angles = positions.astype(F32)[:, None] * frequency[None, :]
    cosine = jnp.cos(angles)[:, None, :]
    sine = jnp.sin(angles)[:, None, :]
    front, back = per_head[..., :half_dim], per_head[..., half_dim:]
    turned = jnp.concatenate([front * cosine - back * sine, back * cosine + front * sine], axis=-1)
    return turned.reshape(row_count, -1)


def attention_kernel(len_ref, q_ref, kn_ref, vn_ref, cart_ref, g_ref, o_ref, grad_ref, kx, vt):
    length = len_ref[0]
    cart = cart_ref.shape[1]
    seq = kn_ref.shape[0]
    heads = q_ref.shape[1] // HD
    scale = HD ** -0.5
    factor = scale * math.log2(math.e)
    nt = (((1,), (1,)), ((), ()))

    live = lax.broadcasted_iota(jnp.int32, (seq, HD), 0) < length
    kx[:cart] = cart_ref[0]
    kx[cart:] = jnp.where(live, kn_ref[...], jnp.broadcast_to(cart_ref[0, 0:1, :], (seq, HD)))
    vt[:HD, :cart] = cart_ref[1].astype(F32).T.astype(BF16)
    vt[:HD, cart:] = jnp.where(live, vn_ref[...].astype(F32), 0.0).T.astype(BF16)
    extra = vt.shape[0] - HD
    spot = lax.broadcasted_iota(jnp.int32, (extra, cart + seq), 1)
    vt[HD:] = jnp.where(spot < cart + length, 1.0, 0.0).astype(BF16)
    grad_ref[...] = jnp.zeros_like(grad_ref)

    for block in range(seq // ROWS):
        before = cart + block * ROWS
        rows = pl.ds(block * ROWS, ROWS)

        @pl.loop(0, heads)
        def _(head):
            columns = pl.ds(pl.multiple_of(head * HD, HD), HD)
            q = q_ref[rows, columns]
            g = g_ref[rows, columns]
            row = block * ROWS + lax.broadcasted_iota(jnp.int32, (ROWS, HD), 0)
            g = jnp.where(row < length, g, jnp.zeros_like(g))
            s_far = lax.dot_general(kx[:before], q, nt, preferred_element_type=F32)
            s_near = lax.dot_general(kx[before:before + ROWS], q, nt, preferred_element_type=F32)
            key = lax.broadcasted_iota(jnp.int32, (ROWS, ROWS), 0)
            query = lax.broadcasted_iota(jnp.int32, (ROWS, ROWS), 1)
            s_near = jnp.where(key <= query, s_near, -jnp.inf)
            top = jnp.maximum(
                jnp.max(s_far, axis=0, keepdims=True), jnp.max(s_near, axis=0, keepdims=True)
            )
            e_far = jnp.exp2((s_far - top) * factor)
            e_near = jnp.exp2((s_near - top) * factor)
            out = jnp.dot(vt[:, :before], e_far.astype(BF16), preferred_element_type=F32)
            out += jnp.dot(vt[:, before:before + ROWS], e_near.astype(BF16), preferred_element_type=F32)
            inverse = 1.0 / out[HD:HD + 1]
            out = out[:HD] * inverse
            o_ref[rows, columns] = out.T.astype(BF16)
            delta = jnp.sum(out * g.astype(F32).T, axis=0, keepdims=True)
            d_prob = lax.dot_general(cart_ref[1], g, nt, preferred_element_type=F32)
            prob = e_far[:cart] * inverse
            d_score = prob * (d_prob - delta)
            grad_ref[1] += jnp.dot(prob.astype(BF16), g, preferred_element_type=F32)
            grad_ref[0] += jnp.dot(d_score.astype(BF16), q, preferred_element_type=F32)

    grad_ref[0] = grad_ref[0] * scale


def attention(length, q, k_new, v_new, cartridge, g):
    vmem = pl.BlockSpec(memory_space=pltpu.VMEM)
    cart, seq = cartridge.shape[1], q.shape[0]
    return pl.pallas_call(
        attention_kernel,
        name="attention",
        out_shape=(
            jax.ShapeDtypeStruct(q.shape, BF16),
            jax.ShapeDtypeStruct((2, cart, HD), F32),
        ),
        in_specs=[pl.BlockSpec(memory_space=pltpu.SMEM)] + [vmem] * 5,
        out_specs=(vmem, vmem),
        scratch_shapes=[
            pltpu.VMEM((cart + seq, HD), BF16),
            pltpu.VMEM((HD + 16, cart + seq), BF16),
        ],
        compiler_params=pltpu.CompilerParams(vmem_limit_bytes=40 << 20),
    )(length, q, k_new, v_new, cartridge, g)


def reduce_kernel(chips, part_ref, sum_ref, from_core, half, to_chips, from_chips, mine, gathered, other,
                  core_send, core_recv, rs_send, rs_recv, ag_send, ag_recv):
    dp, fsdp = lax.axis_index("dp"), lax.axis_index("fsdp")
    chip, core = dp // 2, dp % 2
    rows = part_ref.shape[0] // 2
    share = rows // chips
    sibling = (chip * 2 + (1 - core), fsdp)

    def peer(step):
        return lax.rem(chip + step, chips)

    barrier = pltpu.get_barrier_semaphore()
    pl.semaphore_signal(barrier, inc=1, device_id=sibling, device_id_type=MESH)
    for step in range(1, chips):
        pl.semaphore_signal(barrier, inc=1, device_id=(peer(step) * 2 + core, fsdp), device_id_type=MESH)
    pl.semaphore_wait(barrier, chips)

    def send(src, dst, send_sem, recv_sem, target):
        copy = pltpu.make_async_remote_copy(
            src_ref=src, dst_ref=dst, send_sem=send_sem, recv_sem=recv_sem,
            device_id=target, device_id_type=MESH,
        )
        copy.start()
        return copy

    theirs = pl.ds(pl.multiple_of((1 - core) * rows, rows), rows)
    ours = pl.ds(pl.multiple_of(core * rows, rows), rows)
    copy = send(part_ref.at[theirs], from_core, core_send.at[0], core_recv.at[0], sibling)
    copy.wait()
    half[...] = (part_ref[ours] + from_core[...]).reshape(half.shape)
    to_chips[...] = half[...].astype(BF16)
    copies = [
        send(to_chips.at[peer(step)], from_chips.at[step], rs_send.at[step], rs_recv.at[step],
             (peer(step) * 2 + core, fsdp))
        for step in range(1, chips)
    ]
    total = half[chip]
    for step, copy in zip(range(1, chips), copies):
        copy.wait()
        total += from_chips[step].astype(F32)
    mine[...] = total.astype(BF16)
    gathered[chip] = total.astype(BF16)
    copies = [
        send(mine, gathered.at[chip], ag_send.at[step], ag_recv.at[step], (peer(step) * 2 + core, fsdp))
        for step in range(1, chips)
    ]
    for copy in copies:
        copy.wait()
    copy = send(gathered, other, core_send.at[1], core_recv.at[1], sibling)
    sum_ref[ours] = gathered[...].astype(F32).reshape(rows, HD)
    copy.wait()
    sum_ref[theirs] = other[...].astype(F32).reshape(rows, HD)


def reduce_over_dp(part, n_dp):
    chips = n_dp // 2
    rows = part.shape[0]
    share = rows // 2 // chips
    vmem = pl.BlockSpec(memory_space=pltpu.VMEM)
    dma = pltpu.SemaphoreType.DMA
    return pl.pallas_call(
        functools.partial(reduce_kernel, chips),
        name="reduce_over_dp",
        out_shape=jax.ShapeDtypeStruct(part.shape, F32),
        in_specs=[vmem],
        out_specs=vmem,
        scratch_shapes=[
            pltpu.VMEM((rows // 2, HD), F32),
            pltpu.VMEM((chips, share, HD), F32),
            pltpu.VMEM((chips, share, HD), BF16),
            pltpu.VMEM((chips, share, HD), BF16),
            pltpu.VMEM((share, HD), BF16),
            pltpu.VMEM((chips, share, HD), BF16),
            pltpu.VMEM((chips, share, HD), BF16),
            dma((2,)), dma((2,)), dma((chips,)), dma((chips,)), dma((chips,)), dma((chips,)),
        ],
        compiler_params=pltpu.CompilerParams(collective_id=1, has_side_effects=True),
    )(part)


def on_device(n_dp, hidden_in, lengths, cartridge, norm_gain, w_query, w_keyval, cotangent):
    cart = cartridge.shape[1]
    normed = normalize(hidden_in, norm_gain)
    query_weight = lax.all_gather(w_query, "dp", axis=0, tiled=True)
    pair_weight = lax.all_gather(w_keyval, "dp", axis=0, tiled=True)
    piece = lax.all_gather(normed, "fsdp", axis=0, tiled=True)
    spots = cart + jnp.arange(piece.shape[0])
    query_sum = jnp.dot(piece, query_weight, preferred_element_type=F32)
    pair_sum = jnp.dot(piece, pair_weight.reshape(pair_weight.shape[0], -1), preferred_element_type=F32)
    query = rotate(query_sum, spots, HD).astype(BF16)
    key_new = rotate(pair_sum[:, :HD], spots, HD).astype(BF16)
    value_new = pair_sum[:, HD:].astype(BF16)
    mixed, part = attention(lengths, query, key_new, value_new, cartridge, cotangent)
    summed = reduce_over_dp(part.reshape(-1, HD), n_dp)
    return mixed, summed.reshape(2, cart, HD)


def solution(mesh):
    in_specs = (
        P(("dp", "fsdp"), None),
        P("dp"),
        P(None, None, "fsdp"),
        P(),
        P("dp", "fsdp"),
        P("dp", None, "fsdp"),
        P("dp", "fsdp"),
    )
    out_specs = (P("dp", "fsdp"), P(None, None, "fsdp"))
    return jax.shard_map(
        functools.partial(on_device, mesh.shape["dp"]),
        mesh=mesh, in_specs=in_specs, out_specs=out_specs, check_vma=False,
    )
```

time: 599 us -> 335 us (0.56)
  waiting for transfers between devices: 462 us -> 241 us
  matrix products: 97.9 us -> 14.5 us
  Pallas kernels: 0 us -> 41.6 us
  other arithmetic: 21.4 us -> 13.4 us
  local copies, waits for them, and re-layouts: 1.96 us -> 9.08 us
    psum x1 -> x0, waiting for transfers between devices: 222 us -> none  [on_device(): key_summed, value_summed = lax.psum((key_total, value_total), 'dp')]
    dot_general x42 -> x2, matrix products: 97.9 us -> 14.5 us  [the longest x1 8.24 us: on_device(): query_sum = jnp.dot(piece, query_weight, preferred_element_type=F32)]
    pallas_call x0 -> x2, Pallas kernels: none -> 41.6 us  [the longest x1 22.1 us: reduce_over_dp(): pl.pallas_call(functools.partial(reduce_kernel, chips), name='reduce_over...]
    unnamed x8 -> x10, local copies, waits for them, and re-layouts: 0.67 us -> 7.43 us
  transfers between devices with their start and end apart: 4 -> 3, of which waited for: 4 -> 3; matrix products, arithmetic and copies ran while one was open for 2% -> 4% of each run, Pallas kernels for 0% -> 0%
where the time goes in v1:
time: 335 us; the launch traced here: 334 us
  waiting for transfers between devices  241 us (72%)
  Pallas kernels  41.6 us (12%)
  matrix products  14.5 us (4%)
  between operations  14.5 us (4%)
  other arithmetic  13.4 us (4%)
  local copies, waits for them, and re-layouts  9.08 us (3%)
    all_gather x1, waiting for transfers between devices, on_device(): piece = lax.all_gather(normed, 'fsdp', axis=0, tiled=True)  116 us
    all_gather x1, waiting for transfers between devices, on_device(): pair_weight = lax.all_gather(w_keyval, 'dp', axis=0, tiled=True)  62.4 us
    all_gather x1, waiting for transfers between devices, on_device(): query_weight = lax.all_gather(w_query, 'dp', axis=0, tiled=True)  61.1 us
    pallas_call x1, Pallas kernels, reduce_over_dp(): pl.pallas_call(functools.partial(reduce_kernel, chips), name='reduce_over...  22.1 us
    pallas_call x1, Pallas kernels, attention(): pl.pallas_call(attention_kernel, name='attention', out_shape=(jax.ShapeDt...  19.4 us
    dot_general x1, matrix products, on_device(): query_sum = jnp.dot(piece, query_weight, preferred_element_type=F32)  8.24 us
    unnamed x10, local copies, waits for them, and re-layouts  7.43 us
  transfers between devices with their start and end apart: 3, of which 3 were waited for; matrix products, arithmetic and copies ran while one was open for 4% of the time, Pallas kernels for 0%

profile of v1, /device:TPU:1, one launch (start us, length us, event | category | flops | bytes accessed | tf_op | source)
XLA Modules:
  0.0 334.2 jit_solution(6824520528679490061)
XLA Ops:
  7.2 0.7 all-gather.8.cloned.1.call-update
  7.9 0.0 all-gather.4.cloned.1.call-start
  7.9 1.5 fusion
  9.5 2.5 fusion.2
  12.0 0.0 all-gather.6.cloned.1.call-start
  12.1 0.7 all-gather.6.cloned.1.call-update
  13.4 3.0 multiply_cosine_fusion.1
  16.4 62.4 %all-gather.8.cloned.1.call-done = bf16[4096,2,128]{2,1,0:T(2,128)(2,1)} async-done(((bf16[128,2,128]{2,1,0:T(2,128)(2,1)}), bf16[4096,2,128]{2,1,0:T(2,128)(2,1)}) %all-gather.8.cloned.1.call-update) | async-done | bytes 2097168 | tf_op jit(solution)/shard_map/all_gather | solution.py:199
  78.8 116.1 %all-gather.4.cloned.1.call-done = bf16[1024,4096]{1,0:T(8,128)(2,1)} async-done(((bf16[128,4096]{1,0:T(8,128)(2,1)}), bf16[1024,4096]{1,0:T(8,128)(2,1)}) %all-gather.4.cloned.1.call-update) | async-done | bytes 8388624 | tf_op jit(solution)/shard_map/all_gather | solution.py:200
  194.9 6.3 %fusion.3 = f32[1024,256]{1,0:T(8,128)S(1)} fusion(bf16[1024,4096]{1,0:T(8,128)(2,1)} %all-gather.4.cloned.1.call-done, bf16[512,8,2,128]{3,2,1,0:T(2,128)(2,1)} %bitcast.23), kind=kOutput, calls=%fused_computation.5 | convolution fusion | flops 2147483648 | bytes 11534336 | tf_op jit(solution)/shard_map/dot_general | solution.py:203
  201.3 61.1 %all-gather.6.cloned.1.call-done = bf16[4096,512]{1,0:T(8,128)(2,1)} async-done(((bf16[128,512]{1,0:T(8,128)(2,1)}), bf16[4096,512]{1,0:T(8,128)(2,1)}) %all-gather.6.cloned.1.call-update) | async-done | bytes 4194320 | tf_op jit(solution)/shard_map/all_gather | solution.py:198
  262.4 8.2 %fusion.15 = f32[1024,512]{0,1:T(8,128)S(1)} fusion(bf16[1024,4096]{1,0:T(8,128)(2,1)} %all-gather.4.cloned.1.call-done, bf16[4096,512]{1,0:T(8,128)(2,1)} %all-gather.6.cloned.1.call-done), kind=kOutput, calls=%fused_computation.31 | convolution fusion | flops 4294967296 | bytes 14680064 | tf_op jit(solution)/shard_map/dot_general | solution.py:202
  270.7 1.6 fusion.14
  272.2 1.8 copy.23
  274.1 2.7 copy.24
  276.8 2.4 subtract_convert_fusion
  279.2 1.4 pad_maximum_fusion
  280.7 0.2 copy.32
  280.9 2.4 fusion.11
  283.3 0.1 maximum_bitcast_fusion.kn_ref
  283.5 19.4 %attention.1 = (bf16[1024,512]{1,0:T(8,128)(2,1)}, f32[2,512,128]{2,1,0:T(8,128)S(1)}) custom-call(s32[1]{0:T(128)S(6)} %copy.34.len_ref, bf16[1024,512]{1,0:T(8,128)(2,1)S(1)} %bitcast.18, bf16[1024,128]{1,0:T(8,128)(2,1)S(1)} %maximum_bitcast_fusion.kn_ref, bf16[1024,128]{1,0:T(8,128)(2,1)S(1)} %slice.37.vn_ref, bf16[2,512,128]{2,1,0:T(8,128)(2,1)S(1)} %copy-done.2, ...), custom_call_target="tpu_custom_call" | custom-call | tf_op jit(solution)/shard_map/attention/pallas_call | solution.py:98
  302.9 0.8 copy-done.1
  303.7 22.1 %reduce_over_dp.1 = f32[1024,128]{1,0:T(8,128)} custom-call(f32[1024,128]{1,0:T(8,128)} %bitcast.19), custom_call_target="tpu_custom_call" | custom-call | tf_op jit(solution)/shard_map/reduce_over_dp/pallas_call | solution.py:175
  325.8 1.9 copy.35
  (12 shorter events, 0.2 us)
Async XLA Ops:
  7.2 71.6 %all-gather.8.cloned.1.call-start = ((), (), s32[]{:S(2)}) async-start(), calls=%async_computation.2 | async-start | bytes 2162688 | tf_op jit(solution)/shard_map/all_gather | solution.py:199
  7.9 187.0 %all-gather.4.cloned.1.call-start = ((), (), s32[]{:S(2)}) async-start(), calls=%async_computation | async-start | bytes 9437184 | tf_op jit(solution)/shard_map/all_gather | solution.py:200
  12.0 250.4 %all-gather.6.cloned.1.call-start = ((), (), s32[]{:S(2)}) async-start(), calls=%async_computation.1 | async-start | bytes 4325376 | tf_op jit(solution)/shard_map/all_gather | solution.py:198
  280.7 2.8 copy-start
  280.7 2.8 copy-start.2
  302.9 0.8 copy-start.1
Sparse Core Ops, SparseCore 0:
  9.9 68.8 all-gather.7
  82.0 112.8 all-gather.3
  196.8 65.5 all-gather.5

commit v2 on v1

--- a/solution.py
+++ b/solution.py
@@ -3,6 +3,7 @@
 
 import jax
 import jax.numpy as jnp
+import numpy as np
 from jax import lax
 from jax.experimental import pallas as pl
 from jax.experimental.pallas import tpu as pltpu
@@ -17,24 +18,275 @@
 ROWS = 256
 
 
-def normalize(hidden, norm_gain):
-    floated = hidden.astype(F32)
-    inverse = lax.rsqrt(jnp.mean(floated * floated, axis=-1, keepdims=True) + EPS)
-    return (floated * inverse * norm_gain).astype(BF16)
-
-
-def rotate(matrix, positions, head_dim):
-    row_count = matrix.shape[0]
-    half_dim = head_dim // 2
-    per_head = matrix.reshape(row_count, -1, head_dim)
-    exponent = jnp.arange(half_dim).astype(F32) * (-2.0 / head_dim)
-    frequency = jnp.power(jnp.float32(ROPE_BASE), exponent)
-    angles = positions.astype(F32)[:, None] * frequency[None, :]
-    cosine = jnp.cos(angles)[:, None, :]
-    sine = jnp.sin(angles)[:, None, :]
-    front, back = per_head[..., :half_dim], per_head[..., half_dim:]
-    turned = jnp.concatenate([front * cosine - back * sine, back * cosine + front * sine], axis=-1)
-    return turned.reshape(row_count, -1)
+def project_kernel(hidden_ref, gain_ref, wq_ref, wkv_ref, cos_ref, sin_ref, q_ref, k_ref, v_ref,
+                   xn, wq, wkv, acc_q, acc_kv, q_out, kv_out, q_in, kv_in, local_sem, send_sem, recv_sem):
+    dp, fsdp = lax.axis_index("dp"), lax.axis_index("fsdp")
+    x, y_hi, y_lo, z, c = fsdp // 2, fsdp % 2, dp // 16, (dp // 2) % 8, dp % 2
+    y = y_hi * 2 + y_lo
+    turn = 1 - 2 * c
+
+    def at(dx=0, dy=0, dz=0, other=False):
+        yy = lax.rem(y + dy + 8, 4)
+        return (
+            lax.rem(yy, 2) * 16 + lax.rem(z + dz + 16, 8) * 2 + (1 - c if other else c),
+            lax.rem(x + dx + 8, 4) * 2 + yy // 2,
+        )
+
+    def zs(r):
+        return lax.rem(z + r + 16, 8)
+
+    def ys(dy):
+        yy = lax.rem(y + dy + 8, 4)
+        return yy // 2, lax.rem(yy, 2)
+
+    def xs(dx):
+        return lax.rem(x + dx + 8, 4)
+
+    slots, started = {}, []
+
+    def send(name, ref, target, dst=None):
+        assert name not in slots
+        copy = pltpu.make_async_remote_copy(
+            src_ref=ref, dst_ref=ref if dst is None else dst,
+            send_sem=send_sem.at[len(started)], recv_sem=recv_sem.at[len(started)],
+            device_id=target, device_id_type=MESH,
+        )
+        copy.start()
+        slots[name] = copy
+        started.append(copy)
+
+    def arrived(name):
+        slots[name].wait_recv()
+
+    def wq_at(dy, r, core=None):
+        hi, lo = ys(dy)
+        return wq.at[hi, lo, zs(r), c if core is None else core]
+
+    def wkv_at(dy, r):
+        hi, lo = ys(dy)
+        return wkv.at[hi, lo, zs(r), c]
+
+    own_q = pltpu.make_async_copy(wq_ref, wq_at(0, 0), local_sem.at[0])
+    own_kv = pltpu.make_async_copy(wkv_ref, wkv_at(0, 0), local_sem.at[1])
+    own_q.start()
+    own_kv.start()
+    barrier = pltpu.get_barrier_semaphore()
+    partners = [at(dx=1), at(dx=-1), at(dy=1), at(dy=-1), at(dy=2), at(dz=1), at(dz=-1), at(other=True)]
+    for partner in partners:
+        pl.semaphore_signal(barrier, inc=1, device_id=partner, device_id_type=MESH)
+    pl.semaphore_wait(barrier, len(partners))
+    own_q.wait()
+    own_kv.wait()
+
+    def ticks(i):
+        return {0: [0], 4: [4]}.get(i, [i, -i])
+
+    def wq_from_z(i):
+        if i == 4:
+            arrived(("zq", 4, 0))
+            arrived(("zq", 4, 1))
+        elif i:
+            arrived(("zq", i))
+            arrived(("zq", -i))
+        if i < 3:
+            send(("zq", i + 1), wq_at(0, i), at(dz=-1))
+            send(("zq", -i - 1), wq_at(0, -i), at(dz=1))
+        elif i == 3:
+            send(("zq", 4, 0), wq_at(0, 3).at[pl.ds(0, 64)], at(dz=-1))
+            send(("zq", 4, 1), wq_at(0, -3).at[pl.ds(64, 64)], at(dz=1))
+        for r in ticks(i):
+            send(("yq", -1, r), wq_at(0, r), at(dy=1))
+            send(("yq", 1, r), wq_at(0, r), at(dy=-1))
+
+    def wq_from_y(i):
+        for r in ticks(i):
+            arrived(("yq", -1, r))
+            arrived(("yq", 1, r))
+            way = turn if r in (0, 4) else (1 if r > 0 else -1)
+            send(("yq", 2, r), wq_at(way, r), at(dy=-way))
+
+    def wq_to_core(i):
+        for r in ticks(i):
+            arrived(("yq", 2, r))
+            send(("cq", r), wq.at[:, :, zs(r), c], at(other=True))
+
+    def wkv_from_z(i):
+        if i == 4:
+            arrived(("zk", 4, 0))
+            arrived(("zk", 4, 1))
+        elif i:
+            arrived(("zk", i))
+            arrived(("zk", -i))
+        if i < 3:
+            send(("zk", i + 1), wkv.at[:, :, zs(i), c], at(dz=-1))
+            send(("zk", -i - 1), wkv.at[:, :, zs(-i), c], at(dz=1))
+        elif i == 3:
+            send(("zk", 4, 0), wkv.at[0, :, zs(3), c], at(dz=-1))
+            send(("zk", 4, 1), wkv.at[1, :, zs(-3), c], at(dz=1))
+        for r in ticks(i):
+            send(("ck", r), wkv.at[:, :, zs(r), c], at(other=True))
+
+    def rows_out(i):
+        for r in ticks(i):
+            send(("x", -1, r), xn.at[:, zs(r), x], at(dx=1))
+            send(("x", 1, r), xn.at[:, zs(r), x], at(dx=-1))
+
+    def rows_on(i):
+        for r in ticks(i):
+            arrived(("x", -1, r))
+            arrived(("x", 1, r))
+            send(("x", 2, r, 0), xn.at[0, zs(r), xs(1)], at(dx=-1))
+            send(("x", 2, r, 1), xn.at[1, zs(r), xs(-1)], at(dx=1))
+
+    def multiply(i, halves=(0, 1)):
+        for r in ticks(i):
+            arrived(("cq", r))
+            arrived(("ck", r))
+            arrived(("x", 2, r, 0))
+            arrived(("x", 2, r, 1))
+        for r in ticks(i):
+            spot = zs(r)
+            left = jnp.concatenate([xn[lo, spot].reshape(512, 256) for lo in range(2)], axis=1)
+            for hi in range(2):
+                right = jnp.concatenate([wq[hi, lo, spot].reshape(256, 512) for lo in range(2)], axis=0)
+                term = jnp.dot(left, right, preferred_element_type=F32)
+                acc_q[hi] = term if r == 0 else acc_q[hi] + term
+                right = jnp.concatenate([wkv[hi, lo, spot].reshape(256, 256) for lo in range(2)], axis=0)
+                term = jnp.dot(left, right, preferred_element_type=F32)
+                acc_kv[hi] = term if r == 0 else acc_kv[hi] + term
+
+    wq_from_z(0)
+    send(("yk", -1), wkv_at(0, 0), at(dy=1))
+    send(("yk", 1), wkv_at(0, 0), at(dy=-1))
+    hidden = hidden_ref[...].astype(F32)
+    inverse = lax.rsqrt(jnp.mean(hidden * hidden, axis=-1, keepdims=True) + EPS)
+    for k in range(16):
+        cols = slice(k * 256, (k + 1) * 256)
+        part = hidden_ref[:, cols].astype(F32) * inverse * gain_ref[:, cols]
+        xn[k // 8, k % 8, x] = part.astype(BF16)
+    rows_out(0)
+    rows_out(1)
+    arrived(("yk", -1))
+    arrived(("yk", 1))
+    send(("yk", 2), wkv_at(turn, 0), at(dy=-turn))
+    wq_from_z(1)
+    wq_from_y(0)
+    rows_on(0)
+    rows_out(2)
+    arrived(("yk", 2))
+    wkv_from_z(0)
+    wq_to_core(0)
+    wq_from_z(2)
+    wq_from_y(1)
+    rows_on(1)
+    rows_out(3)
+    multiply(0)
+    wkv_from_z(1)
+    wq_from_z(3)
+    wq_to_core(1)
+    wq_from_y(2)
+    rows_on(2)
+    rows_out(4)
+    multiply(1)
+    wkv_from_z(2)
+    wq_from_z(4)
+    wq_to_core(2)
+    wq_from_y(3)
+    rows_on(3)
+    multiply(2)
+    wkv_from_z(3)
+    wq_to_core(3)
+    wq_from_y(4)
+    rows_on(4)
+    multiply(3)
+    wkv_from_z(4)
+    wq_to_core(4)
+    multiply(4)
+
+    cos = cos_ref[:, y_hi].reshape(512, HD)
+    sin = sin_ref[:, y_hi].reshape(512, HD)
+
+    def turned(part):
+        return (part * cos + pltpu.roll(part, HD // 2, 1) * sin).astype(BF16)
+
+    def finish_kv(hi, put):
+        put(0, turned(acc_kv[hi, :, :HD]).reshape(4, 128, HD))
+        put(1, acc_kv[hi, :, HD:].astype(BF16).reshape(4, 128, HD))
+
+    def finish_q(hi, put):
+        for head in range(4):
+            cols = slice(head * HD, (head + 1) * HD)
+            put(cols, turned(acc_q[hi, :, cols]).reshape(4, 128, HD))
+
+    def put_kv_out(i, value):
+        kv_out[i] = value
+
+    def put_q_out(cols, value):
+        q_out[:, :, cols] = value
+
+    def put_kv(i, value):
+        (k_ref, v_ref)[i][:, y_hi] = value
+
+    def put_q(cols, value):
+        q_ref[:, y_hi, :, cols] = value
+
+    finish_kv(1 - y_hi, put_kv_out)
+    send("kv", kv_out, at(dy=2), kv_in)
+    finish_q(1 - y_hi, put_q_out)
+    send("q", q_out, at(dy=2), q_in)
+    finish_kv(y_hi, put_kv)
+    finish_q(y_hi, put_q)
+    arrived("kv")
+    k_ref[:, 1 - y_hi] = kv_in[0]
+    v_ref[:, 1 - y_hi] = kv_in[1]
+    arrived("q")
+    q_ref[:, 1 - y_hi] = q_in[...]
+    for copy in started:
+        copy.wait_send()
+
+
+def rope_tables(cart, seq):
+    frequency = np.power(np.float32(ROPE_BASE), np.arange(HD // 2, dtype=np.float32) * np.float32(-2.0 / HD))
+    angles = (cart + np.arange(seq, dtype=np.float32))[:, None] * frequency.astype(np.float32)[None, :]
+    cos, sin = np.cos(angles), np.sin(angles)
+    shape = (seq // 256, 2, 128, HD)
+    return (
+        np.concatenate([cos, cos], axis=1).astype(np.float32).reshape(shape),
+        np.concatenate([-sin, sin], axis=1).astype(np.float32).reshape(shape),
+    )
+
+
+def project(hidden, gain, w_query, w_keyval, cart):
+    vmem, hbm = pl.BlockSpec(memory_space=pltpu.VMEM), pl.BlockSpec(memory_space=pl.ANY)
+    cos, sin = rope_tables(cart, 1024)
+    copies = 160
+    q, k, v = pl.pallas_call(
+        project_kernel,
+        name="project",
+        out_shape=(
+            jax.ShapeDtypeStruct((4, 2, 128, 512), BF16),
+            jax.ShapeDtypeStruct((4, 2, 128, HD), BF16),
+            jax.ShapeDtypeStruct((4, 2, 128, HD), BF16),
+        ),
+        in_specs=[vmem, vmem, hbm, hbm, vmem, vmem],
+        out_specs=(vmem,) * 3,
+        scratch_shapes=[
+            pltpu.VMEM((2, 8, 4, 128, 256), BF16),
+            pltpu.VMEM((2, 2, 8, 2, 128, 512), BF16),
+            pltpu.VMEM((2, 2, 8, 2, 128, 256), BF16),
+            pltpu.VMEM((2, 512, 512), F32),
+            pltpu.VMEM((2, 512, 256), F32),
+            pltpu.VMEM((4, 128, 512), BF16),
+            pltpu.VMEM((2, 4, 128, HD), BF16),
+            pltpu.VMEM((4, 128, 512), BF16),
+            pltpu.VMEM((2, 4, 128, HD), BF16),
+            pltpu.SemaphoreType.DMA((2,)),
+            pltpu.SemaphoreType.DMA((copies,)),
+            pltpu.SemaphoreType.DMA((copies,)),
+        ],
+        compiler_params=pltpu.CompilerParams(collective_id=0, has_side_effects=True, vmem_limit_bytes=48 << 20),
+    )(hidden, gain.reshape(1, -1), w_query, w_keyval.reshape(128, 256), cos, sin)
+    return q.reshape(1024, 512), k.reshape(1024, HD), v.reshape(1024, HD)
 
 
 def attention_kernel(len_ref, q_ref, kn_ref, vn_ref, cart_ref, g_ref, o_ref, grad_ref, kx, vt):
@@ -194,16 +446,7 @@
 
 def on_device(n_dp, hidden_in, lengths, cartridge, norm_gain, w_query, w_keyval, cotangent):
     cart = cartridge.shape[1]
-    normed = normalize(hidden_in, norm_gain)
-    query_weight = lax.all_gather(w_query, "dp", axis=0, tiled=True)
-    pair_weight = lax.all_gather(w_keyval, "dp", axis=0, tiled=True)
-    piece = lax.all_gather(normed, "fsdp", axis=0, tiled=True)
-    spots = cart + jnp.arange(piece.shape[0])
-    query_sum = jnp.dot(piece, query_weight, preferred_element_type=F32)
-    pair_sum = jnp.dot(piece, pair_weight.reshape(pair_weight.shape[0], -1), preferred_element_type=F32)
-    query = rotate(query_sum, spots, HD).astype(BF16)
-    key_new = rotate(pair_sum[:, :HD], spots, HD).astype(BF16)
-    value_new = pair_sum[:, HD:].astype(BF16)
+    query, key_new, value_new = project(hidden_in, norm_gain, w_query, w_keyval, cart)
     mixed, part = attention(lengths, query, key_new, value_new, cartridge, cotangent)
     summed = reduce_over_dp(part.reshape(-1, HD), n_dp)
     return mixed, summed.reshape(2, cart, HD)

time: 335 us -> 129 us (0.39)
  waiting for transfers between devices: 241 us -> 0 us
  Pallas kernels: 41.6 us -> 120 us
  matrix products: 14.5 us -> 0 us
  other arithmetic: 13.4 us -> 0 us
  between operations: 14.5 us -> 1.38 us
    all_gather x3 -> x0, waiting for transfers between devices: 240 us -> none  [the longest x1 116 us: on_device(): piece = lax.all_gather(normed, 'fsdp', axis=0, tiled=True)]
    pallas_call x0 -> x1, Pallas kernels: none -> 77.1 us  [project(): pl.pallas_call(project_kernel, name='project', out_shape=(jax.ShapeDtypeS...]
    dot_general x2 -> x0, matrix products: 14.5 us -> none  [the longest x1 8.24 us: on_device(): query_sum = jnp.dot(piece, query_weight, preferred_element_type=F32)]
    another operation x2 -> x0, other arithmetic: 4.82 us -> none
    unnamed x10 -> x18, local copies, waits for them, and re-layouts: 7.43 us -> 7.54 us
  transfers between devices with their start and end apart: 3 -> 0, of which waited for: 3 -> 0; matrix products, arithmetic and copies ran while one was open for 4% -> 0% of each run, Pallas kernels for 0% -> 0%
where the time goes in v2:
time: 129 us
  Pallas kernels  120 us (93%)
  local copies, waits for them, and re-layouts  7.54 us (6%)
  between operations  1.38 us (1%)
    pallas_call x1, Pallas kernels, project(): pl.pallas_call(project_kernel, name='project', out_shape=(jax.ShapeDtypeS...  77.1 us
    pallas_call x1, Pallas kernels, reduce_over_dp(): pl.pallas_call(functools.partial(reduce_kernel, chips), name='reduce_over...  23.3 us
    pallas_call x1, Pallas kernels, attention(): pl.pallas_call(attention_kernel, name='attention', out_shape=(jax.ShapeDt...  19.4 us
    unnamed x18, local copies, waits for them, and re-layouts  7.54 us

profile of v2, /device:TPU:1, one launch (start us, length us, event | category | flops | bytes accessed | tf_op | source)
XLA Modules:
  0.0 128.8 jit_solution(3811809775736974601)
XLA Ops:
  0.6 0.0 copy-start.6
  1.3 0.9 copy.13
  2.2 0.0 copy-done.6
  2.2 0.0 copy-start.1
  2.2 1.2 copy-done.1
  3.4 0.0 copy-start.3
  3.4 1.0 copy-done.3
  4.5 0.0 copy-start.4
  4.5 1.0 copy-done.4
  5.5 0.0 copy-start.7
  5.5 0.7 copy-done.7
  6.2 0.0 copy-start
  6.2 0.0 copy-start.5
  6.2 77.1 %project.1 = (bf16[4,2,128,512]{3,2,1,0:T(8,128)(2,1)S(1)}, bf16[4,2,128,128]{3,2,1,0:T(8,128)(2,1)S(1)}, bf16[4,2,128,128]{3,2,1,0:T(8,128)(2,1)S(1)}) custom-call(bf16[128,4096]{1,0:T(8,128)(2,1)S(1)} %copy-done.1, f32[1,4096]{1,0:T(1,128)S(1)} %bitcast.15, bf16[128,512]{1,0:T(8,128)(2,1)S(1)} %copy-done.6, bf16[128,256]{1,0:T(8,128)(2,1)S(1)} %bitcast.14, ...), custom_call_target="tpu_custom_call" | custom-call | tf_op jit(solution)/shard_map/project/pallas_call | solution.py:263
  83.4 0.0 copy-done
  83.4 0.0 copy-done.5
  83.4 19.4 %attention.1 = (bf16[1024,512]{1,0:T(8,128)(2,1)}, f32[2,512,128]{2,1,0:T(8,128)S(1)}) custom-call(s32[1]{0:T(128)S(6)} %copy.15.len_ref, bf16[1024,512]{1,0:T(8,128)(2,1)S(1)} %bitcast.10, bf16[1024,128]{1,0:T(8,128)(2,1)S(1)} %bitcast.12, bf16[1024,128]{1,0:T(8,128)(2,1)S(1)} %bitcast.13, bf16[2,512,128]{2,1,0:T(8,128)(2,1)S(1)} %copy-done.5, ...), custom_call_target="tpu_custom_call" | custom-call | tf_op jit(solution)/shard_map/attention/pallas_call | solution.py:350
  102.8 0.0 copy-start.2
  102.8 0.8 copy-done.2
  103.6 23.3 %reduce_over_dp.1 = f32[1024,128]{1,0:T(8,128)} custom-call(f32[1024,128]{1,0:T(8,128)} %bitcast.11), custom_call_target="tpu_custom_call" | custom-call | tf_op jit(solution)/shard_map/reduce_over_dp/pallas_call | solution.py:427
  126.9 1.9 %copy.16 = f32[2,512,128]{2,1,0:T(8,128)} copy(f32[2,512,128]{2,1,0:T(8,128)} %bitcast.16) | data formatting | bytes 1048576
Async XLA Ops:
  0.6 1.5 %copy-start.6 = (bf16[128,512]{1,0:T(8,128)(2,1)S(1)}, bf16[128,512]{1,0:T(8,128)(2,1)}, u32[]{:S(2)}) copy-start(bf16[128,512]{1,0:T(8,128)(2,1)} %wq_ref.1) | copy-start | bytes 393220
  2.2 1.2 copy-start.1
  3.4 1.0 copy-start.3
  4.5 1.0 copy-start.4
  5.5 0.7 copy-start.7
  6.2 77.1 %copy-start = (bf16[1024,512]{1,0:T(8,128)(2,1)S(1)}, bf16[1024,512]{1,0:T(8,128)(2,1)}, u32[]{:S(2)}) copy-start(bf16[1024,512]{1,0:T(8,128)(2,1)} %g_ref.1) | copy-start | bytes 3145732
  6.2 77.1 %copy-start.5 = (bf16[2,512,128]{2,1,0:T(8,128)(2,1)S(1)}, bf16[2,512,128]{2,1,0:T(8,128)(2,1)}, u32[]{:S(2)}) copy-start(bf16[2,512,128]{2,1,0:T(8,128)(2,1)} %cart_ref.1) | copy-start | bytes 786436
  102.8 0.8 copy-start.2

commit v3 on v2

v3 whole, which is shorter than its diff:
```python
import functools
import math

import jax
import jax.numpy as jnp
import numpy as np
from jax import lax
from jax.experimental import pallas as pl
from jax.experimental.pallas import tpu as pltpu
from jax.sharding import PartitionSpec as P

HD = 128
MESH = pl.DeviceIdType.MESH
EPS = 1e-05
ROPE_BASE = 500000.0
F32 = jnp.float32
BF16 = jnp.bfloat16
NT = (((1,), (1,)), ((), ()))
CHIPS = 16


def layer_kernel(len_ref, hidden_hbm, gain_hbm, wq_ref, wkv_ref, cos_hbm, sin_hbm, cart_hbm, g_hbm,
                 mixed_ref, sum_ref,
                 hidden_ref, gain_ref, cos_ref, sin_ref, cart_ref, g_ref,
                 xn, wq, wkv, acc_q, acc_kv, q_out, kv_out, q_in, kv_in, q_own, kv_own,
                 kx, vt, e_keep, d_keep, top_keep, grad, from_core, half, to_chips, from_chips, gathered, other,
                 local_sem, send_sem, recv_sem):
    dp, fsdp = lax.axis_index("dp"), lax.axis_index("fsdp")
    x, y_hi, y_lo, z, c = fsdp // 2, fsdp % 2, dp // 16, (dp // 2) % 8, dp % 2
    chip = dp // 2
    y = y_hi * 2 + y_lo
    turn = 1 - 2 * c
    length = len_ref[0]
    cart, seq = cart_ref.shape[1], 1024
    scale = HD ** -0.5
    factor = scale * math.log2(math.e)

    def at(dx=0, dy=0, dz=0, other=False):
        yy = lax.rem(y + dy + 8, 4)
        return (
            lax.rem(yy, 2) * 16 + lax.rem(z + dz + 16, 8) * 2 + (1 - c if other else c),
            lax.rem(x + dx + 8, 4) * 2 + yy // 2,
        )

    def peer(step):
        return lax.rem(chip + step, CHIPS)

    def zs(r):
        return lax.rem(z + r + 16, 8)

    def ys(dy):
        yy = lax.rem(y + dy + 8, 4)
        return yy // 2, lax.rem(yy, 2)

    def xs(dx):
        return lax.rem(x + dx + 8, 4)

    slots, started = {}, []

    def send(name, ref, target, dst=None):
        assert name not in slots
        copy = pltpu.make_async_remote_copy(
            src_ref=ref, dst_ref=ref if dst is None else dst,
            send_sem=send_sem.at[len(started)], recv_sem=recv_sem.at[len(started)],
            device_id=target, device_id_type=MESH,
        )
        copy.start()
        slots[name] = copy
        started.append(copy)

    def arrived(name):
        slots[name].wait_recv()

    def wq_at(dy, r, core=None):
        hi, lo = ys(dy)
        return wq.at[hi, lo, zs(r), c if core is None else core]

    def wkv_at(dy, r):
        hi, lo = ys(dy)
        return wkv.at[hi, lo, zs(r), c]

    local = []
    for n, (ref, dst) in enumerate([
        (wq_ref, wq_at(0, 0)), (wkv_ref, wkv_at(0, 0)), (hidden_hbm, hidden_ref), (gain_hbm, gain_ref),
        (cos_hbm.at[:, y_hi], cos_ref), (sin_hbm.at[:, y_hi], sin_ref), (cart_hbm, cart_ref), (g_hbm, g_ref),
    ]):
        copy = pltpu.make_async_copy(ref, dst, local_sem.at[n])
        copy.start()
        local.append(copy)
    barrier = pltpu.get_barrier_semaphore()
    partners = [at(dx=1), at(dx=-1), at(dy=1), at(dy=-1), at(dy=2), at(dz=1), at(dz=-1), at(other=True)]
    peers = [(peer(step) * 2 + c, fsdp) for step in range(1, CHIPS)]
    for partner in partners + peers:
        pl.semaphore_signal(barrier, inc=1, device_id=partner, device_id_type=MESH)
    pl.semaphore_wait(barrier, len(partners) + len(peers))
    local[0].wait()
    local[1].wait()

    def ticks(i):
        return {0: [0], 4: [4]}.get(i, [i, -i])

    def wq_from_z(i):
        if i == 4:
            arrived(("zq", 4, 0))
            arrived(("zq", 4, 1))
        elif i:
            arrived(("zq", i))
            arrived(("zq", -i))
        if i < 3:
            send(("zq", i + 1), wq_at(0, i), at(dz=-1))
            send(("zq", -i - 1), wq_at(0, -i), at(dz=1))
        elif i == 3:
            send(("zq", 4, 0), wq_at(0, 3).at[pl.ds(0, 64)], at(dz=-1))
            send(("zq", 4, 1), wq_at(0, -3).at[pl.ds(64, 64)], at(dz=1))
        for r in ticks(i):
            send(("yq", -1, r), wq_at(0, r), at(dy=1))
            send(("yq", 1, r), wq_at(0, r), at(dy=-1))

    def wq_from_y(i):
        for r in ticks(i):
            arrived(("yq", -1, r))
            arrived(("yq", 1, r))
            way = turn if r in (0, 4) else (1 if r > 0 else -1)
            send(("yq", 2, r), wq_at(way, r), at(dy=-way))

    def wq_to_core(i):
        for r in ticks(i):
            arrived(("yq", 2, r))
            send(("cq", r), wq.at[:, :, zs(r), c], at(other=True))

    def wkv_from_z(i):
        if i == 4:
            arrived(("zk", 4, 0))
            arrived(("zk", 4, 1))
        elif i:
            arrived(("zk", i))
            arrived(("zk", -i))
        if i < 3:
            send(("zk", i + 1), wkv.at[:, :, zs(i), c], at(dz=-1))
            send(("zk", -i - 1), wkv.at[:, :, zs(-i), c], at(dz=1))
        elif i == 3:
            send(("zk", 4, 0), wkv.at[0, :, zs(3), c], at(dz=-1))
            send(("zk", 4, 1), wkv.at[1, :, zs(-3), c], at(dz=1))
        for r in ticks(i):
            send(("ck", r), wkv.at[:, :, zs(r), c], at(other=True))

    def rows_out(i):
        for r in ticks(i):
            send(("x", -1, r), xn.at[:, zs(r), x], at(dx=1))
            send(("x", 1, r), xn.at[:, zs(r), x], at(dx=-1))

    def rows_on(i):
        for r in ticks(i):
            arrived(("x", -1, r))
            arrived(("x", 1, r))
            send(("x", 2, r, 0), xn.at[0, zs(r), xs(1)], at(dx=-1))
            send(("x", 2, r, 1), xn.at[1, zs(r), xs(-1)], at(dx=1))

    def multiply(i, halves=(0, 1)):
        for r in ticks(i):
            arrived(("cq", r))
            arrived(("ck", r))
            arrived(("x", 2, r, 0))
            arrived(("x", 2, r, 1))
        for r in ticks(i):
            spot = zs(r)
            left = jnp.concatenate([xn[lo, spot].reshape(512, 256) for lo in range(2)], axis=1)
            for hi in range(2):
                right = jnp.concatenate([wq[hi, lo, spot].reshape(256, 512) for lo in range(2)], axis=0)
                term = jnp.dot(left, right, preferred_element_type=F32)
                acc_q[hi] = term if r == 0 else acc_q[hi] + term
                right = jnp.concatenate([wkv[hi, lo, spot].reshape(256, 256) for lo in range(2)], axis=0)
                term = jnp.dot(left, right, preferred_element_type=F32)
                acc_kv[hi] = term if r == 0 else acc_kv[hi] + term

    wq_from_z(0)
    send(("yk", -1), wkv_at(0, 0), at(dy=1))
    send(("yk", 1), wkv_at(0, 0), at(dy=-1))
    local[2].wait()
    local[3].wait()
    hidden = hidden_ref[...].astype(F32)
    inverse = lax.rsqrt(jnp.mean(hidden * hidden, axis=-1, keepdims=True) + EPS)
    for k in range(16):
        cols = slice(k * 256, (k + 1) * 256)
        part = hidden_ref[:, cols].astype(F32) * inverse * gain_ref[:, cols]
        xn[k // 8, k % 8, x] = part.astype(BF16)
    rows_out(0)
    rows_out(1)
    for copy in local[4:]:
        copy.wait()
    kx[:cart] = cart_ref[0]
    vt[:HD, :cart] = cart_ref[1].astype(F32).T.astype(BF16)
    spot = lax.broadcasted_iota(jnp.int32, (vt.shape[0] - HD, cart + seq), 1)
    vt[HD:] = jnp.where(spot < cart + length, 1.0, 0.0).astype(BF16)
    grad[...] = jnp.zeros_like(grad)
    arrived(("yk", -1))
    arrived(("yk", 1))
    send(("yk", 2), wkv_at(turn, 0), at(dy=-turn))
    wq_from_z(1)
    wq_from_y(0)
    rows_on(0)
    rows_out(2)
    arrived(("yk", 2))
    wkv_from_z(0)
    wq_to_core(0)
    wq_from_z(2)
    wq_from_y(1)
    rows_on(1)
    rows_out(3)
    multiply(0)
    wkv_from_z(1)
    wq_from_z(3)
    wq_to_core(1)
    wq_from_y(2)
    rows_on(2)
    rows_out(4)
    multiply(1)
    wkv_from_z(2)
    wq_from_z(4)
    wq_to_core(2)
    wq_from_y(3)
    rows_on(3)
    multiply(2)
    wkv_from_z(3)
    wq_to_core(3)
    wq_from_y(4)
    rows_on(4)
    multiply(3)
    wkv_from_z(4)
    wq_to_core(4)
    multiply(4)


    cos, sin = cos_ref[...].reshape(512, HD), sin_ref[...].reshape(512, HD)

    def turned(part):
        return (part * cos + pltpu.roll(part, HD // 2, 1) * sin).astype(BF16).reshape(4, HD, HD)

    def finish_kv(hi, out):
        out[0] = turned(acc_kv[hi, :, :HD])
        out[1] = acc_kv[hi, :, HD:].astype(BF16).reshape(4, HD, HD)

    theirs = 1 - y_hi
    finish_kv(theirs, kv_out)
    send("kv", kv_out, at(dy=2), kv_in)
    first_q = len(started)
    for head in range(4):
        q_out[head] = turned(acc_q[theirs, :, head * HD:(head + 1) * HD])
        send(("q", head), q_out.at[head], at(dy=2), q_in.at[head])
    for head in range(4):
        q_own[head] = turned(acc_q[y_hi, :, head * HD:(head + 1) * HD])

    def rows_of(hi):
        lane = lax.broadcasted_iota(jnp.int32, (1, 2 * HD), 1)
        return (lane // HD) * (2 * HD) + hi * HD + lax.rem(lane, HD)

    def grad_rows(head, j, hi):
        columns = pl.ds(pl.multiple_of(head * HD, HD), HD)
        g = g_ref[2 * j:2 * j + 2, hi, :, columns].reshape(2 * HD, HD)
        row = lax.broadcasted_iota(jnp.int32, (2 * HD, HD), 0)
        row = 4 * j * HD + (row // HD) * (2 * HD) + hi * HD + lax.rem(row, HD)
        return jnp.where(row < length, g, jnp.zeros_like(g))

    def cart_part(q, g):
        scores = lax.dot_general(kx[:cart], q, NT, preferred_element_type=F32)
        top = jnp.max(scores, axis=0, keepdims=True)
        d_prob = lax.dot_general(cart_ref[1], g, NT, preferred_element_type=F32)
        return jnp.exp2((scores - top) * factor), top, d_prob

    def new_part(head, j, hi, q, g, e_cart, top_cart, d_prob):
        near = cart + 4 * j * HD
        end = near + 4 * HD
        s_near = lax.dot_general(kx[near:end], q, NT, preferred_element_type=F32)
        key = lax.broadcasted_iota(jnp.int32, s_near.shape, 0)
        s_near = jnp.where(key <= rows_of(hi), s_near, -jnp.inf)
        top = jnp.maximum(top_cart, jnp.max(s_near, axis=0, keepdims=True))
        if j:
            s_far = lax.dot_general(kx[cart:near], q, NT, preferred_element_type=F32)
            top = jnp.maximum(top, jnp.max(s_far, axis=0, keepdims=True))
        shrink = jnp.exp2((top_cart - top) * factor)
        e_near = jnp.exp2((s_near - top) * factor).astype(BF16)
        out = jnp.dot(vt[:, :cart], e_cart.astype(BF16), preferred_element_type=F32) * shrink
        out += jnp.dot(vt[:, near:end], e_near, preferred_element_type=F32)
        if j:
            e_far = jnp.exp2((s_far - top) * factor).astype(BF16)
            out += jnp.dot(vt[:, cart:near], e_far, preferred_element_type=F32)
        inverse = 1.0 / out[HD:HD + 1]
        out = out[:HD] * inverse
        columns = pl.ds(pl.multiple_of(head * HD, HD), HD)
        mixed_ref[2 * j:2 * j + 2, hi, :, columns] = out.T.astype(BF16).reshape(2, HD, HD)
        delta = jnp.sum(out * g.astype(F32).T, axis=0, keepdims=True)
        prob = e_cart * (shrink * inverse)
        d_score = prob * (d_prob - delta)
        grad[1] += jnp.dot(prob.astype(BF16), g, preferred_element_type=F32)
        grad[0] += jnp.dot(d_score.astype(BF16), q, preferred_element_type=F32)

    @pl.loop(0, 4)
    def _(head):
        for j in range(2):
            q = q_own[head, 2 * j:2 * j + 2].reshape(2 * HD, HD)
            e_cart, top, d_prob = cart_part(q, grad_rows(head, j, y_hi))
            e_keep[head, j] = e_cart
            d_keep[head, j] = d_prob
            top_keep[head, j] = top

    finish_kv(y_hi, kv_own)
    arrived("kv")
    for n in range(4):
        for hi, blocks in ((y_hi, kv_own), (theirs, kv_in)):
            first = pl.multiple_of((2 * n + hi) * HD, HD)
            live = first + lax.broadcasted_iota(jnp.int32, (HD, HD), 0) < length
            spare = jnp.broadcast_to(cart_ref[0, 0:1, :], (HD, HD))
            kx[pl.ds(cart + first, HD)] = jnp.where(live, blocks[0, n], spare)
            values = jnp.where(live, blocks[1, n].astype(F32), 0.0)
            vt[:HD, pl.ds(cart + first, HD)] = values.T.astype(BF16)

    @pl.loop(0, 4)
    def _(head):
        for j in range(2):
            q = q_own[head, 2 * j:2 * j + 2].reshape(2 * HD, HD)
            g = grad_rows(head, j, y_hi)
            new_part(head, j, y_hi, q, g, e_keep[head, j], top_keep[head, j], d_keep[head, j])

    @pl.loop(0, 4)
    def _(head):
        pltpu.make_async_remote_copy(
            src_ref=q_out.at[head], dst_ref=q_in.at[head], send_sem=send_sem.at[first_q + head],
            recv_sem=recv_sem.at[first_q + head], device_id=at(dy=2), device_id_type=MESH,
        ).wait_recv()
        for j in range(2):
            q = q_in[head, 2 * j:2 * j + 2].reshape(2 * HD, HD)
            g = grad_rows(head, j, theirs)
            new_part(head, j, theirs, q, g, *cart_part(q, g))

    rows = cart
    grad[0] = grad[0] * scale
    send("core_sum", grad.at[1 - c], at(other=True), from_core)
    arrived("core_sum")
    half[...] = (grad[c] + from_core[...]).reshape(half.shape)
    to_chips[...] = half[...].astype(BF16)
    for step in range(1, CHIPS):
        send(("rs", step), to_chips.at[peer(step)], peers[step - 1], from_chips.at[step])
    total = half[chip]
    for step in range(1, CHIPS):
        arrived(("rs", step))
        total += from_chips[step].astype(F32)
    gathered[chip] = total.astype(BF16)
    for step in range(1, CHIPS):
        send(("ag", step), gathered.at[chip], peers[step - 1])
    for step in range(1, CHIPS):
        arrived(("ag", step))
    send("core_back", gathered, at(other=True), other)
    sum_ref[c] = gathered[...].reshape(rows, HD)
    arrived("core_back")
    sum_ref[1 - c] = other[...].reshape(rows, HD)
    for copy in started:
        copy.wait_send()


def rope_tables(cart, seq):
    frequency = np.power(np.float32(ROPE_BASE), np.arange(HD // 2, dtype=np.float32) * np.float32(-2.0 / HD))
    angles = (cart + np.arange(seq, dtype=np.float32))[:, None] * frequency.astype(np.float32)[None, :]
    cos, sin = np.cos(angles), np.sin(angles)
    shape = (seq // 256, 2, 128, HD)
    return (
        np.concatenate([cos, cos], axis=1).astype(np.float32).reshape(shape),
        np.concatenate([-sin, sin], axis=1).astype(np.float32).reshape(shape),
    )


def tail_kernel(mixed_ref, sum_ref, mixed_out, sum_out, sem):
    copy = pltpu.make_async_copy(mixed_ref, mixed_out, sem)
    copy.start()
    sum_out[...] = sum_ref[...].astype(F32)
    copy.wait()


def on_device(hidden_in, lengths, cartridge, norm_gain, w_query, w_keyval, cotangent):
    cart = cartridge.shape[1]
    vmem, hbm = pl.BlockSpec(memory_space=pltpu.VMEM), pl.BlockSpec(memory_space=pltpu.HBM)
    cos, sin = rope_tables(cart, 1024)
    copies, share = 200, cart // CHIPS
    mixed, summed = pl.pallas_call(
        layer_kernel,
        name="layer",
        out_shape=(
            jax.ShapeDtypeStruct((4, 2, 128, 512), BF16),
            jax.ShapeDtypeStruct((2, cart, HD), BF16),
        ),
        in_specs=[pl.BlockSpec(memory_space=pltpu.SMEM)] + [hbm] * 8,
        out_specs=(vmem,) * 2,
        scratch_shapes=[
            pltpu.VMEM((128, 4096), BF16),
            pltpu.VMEM((1, 4096), F32),
            pltpu.VMEM((4, 128, HD), F32),
            pltpu.VMEM((4, 128, HD), F32),
            pltpu.VMEM((2, cart, HD), BF16),
            pltpu.VMEM((4, 2, 128, 512), BF16),
            pltpu.VMEM((2, 8, 4, 128, 256), BF16),
            pltpu.VMEM((2, 2, 8, 2, 128, 512), BF16),
            pltpu.VMEM((2, 2, 8, 2, 128, 256), BF16),
            pltpu.VMEM((2, 512, 512), F32),
            pltpu.VMEM((2, 512, 256), F32),
            pltpu.VMEM((4, 4, 128, HD), BF16),
            pltpu.VMEM((2, 4, 128, HD), BF16),
            pltpu.VMEM((4, 4, 128, HD), BF16),
            pltpu.VMEM((2, 4, 128, HD), BF16),
            pltpu.VMEM((4, 4, 128, HD), BF16),
            pltpu.VMEM((2, 4, 128, HD), BF16),
            pltpu.VMEM((cart + 1024, HD), BF16),
            pltpu.VMEM((HD + 16, cart + 1024), BF16),
            pltpu.VMEM((4, 2, cart, 256), F32),
            pltpu.VMEM((4, 2, cart, 256), F32),
            pltpu.VMEM((4, 2, 1, 256), F32),
            pltpu.VMEM((2, cart, HD), F32),
            pltpu.VMEM((cart, HD), F32),
            pltpu.VMEM((CHIPS, share, HD), F32),
            pltpu.VMEM((CHIPS, share, HD), BF16),
            pltpu.VMEM((CHIPS, share, HD), BF16),
            pltpu.VMEM((CHIPS, share, HD), BF16),
            pltpu.VMEM((CHIPS, share, HD), BF16),
            pltpu.SemaphoreType.DMA((8,)),
            pltpu.SemaphoreType.DMA((copies,)),
            pltpu.SemaphoreType.DMA((copies,)),
        ],
        compiler_params=pltpu.CompilerParams(collective_id=0, has_side_effects=True, vmem_limit_bytes=60 << 20),
    )(lengths, hidden_in, norm_gain.reshape(1, -1), w_query, w_keyval.reshape(128, 256), cos, sin, cartridge,
      cotangent.reshape(4, 2, 128, 512))
    mixed, summed = pl.pallas_call(
        tail_kernel,
        name="tail",
        out_shape=(
            jax.ShapeDtypeStruct(mixed.shape, BF16),
            jax.ShapeDtypeStruct(summed.shape, F32),
        ),
        in_specs=[vmem, vmem],
        out_specs=(pl.BlockSpec(memory_space=pl.ANY), vmem),
        scratch_shapes=[pltpu.SemaphoreType.DMA],
    )(mixed, summed)
    return mixed.reshape(1024, 512), summed


def solution(mesh):
    in_specs = (
        P(("dp", "fsdp"), None),
        P("dp"),
        P(None, None, "fsdp"),
        P(),
        P("dp", "fsdp"),
        P("dp", None, "fsdp"),
        P("dp", "fsdp"),
    )
    out_specs = (P("dp", "fsdp"), P(None, None, "fsdp"))
    return jax.shard_map(on_device, mesh=mesh, in_specs=in_specs, out_specs=out_specs, check_vma=False)
```

time: 129 us -> 109 us (0.84)
  Pallas kernels: 120 us -> 106 us
  local copies, waits for them, and re-layouts: 7.54 us -> 1.48 us
    pallas_call x3 -> x2, Pallas kernels: 120 us -> 106 us  [the longest x1 103 us: on_device(): pl.pallas_call(layer_kernel, name='layer', out_shape=(jax.ShapeDtypeStruc...]
    unnamed x18 -> x1, local copies, waits for them, and re-layouts: 7.54 us -> 1.48 us
where the time goes in v3:
time: 109 us
  Pallas kernels  106 us (97%)
  local copies, waits for them, and re-layouts  1.48 us (1%)
  between operations  1.28 us (1%)
    pallas_call x1, Pallas kernels, on_device(): pl.pallas_call(layer_kernel, name='layer', out_shape=(jax.ShapeDtypeStruc...  103 us
    pallas_call x1, Pallas kernels, on_device(): pl.pallas_call(tail_kernel, name='tail', out_shape=(jax.ShapeDtypeStruct(...  3.04 us

profile of v3, /device:TPU:1, one launch (start us, length us, event | category | flops | bytes accessed | tf_op | source)
XLA Modules:
  0.0 108.7 jit_solution(12778931331193291550)
XLA Ops:
  1.3 1.5 %copy.13 = bf16[16,8,2,128]{3,1,2,0:T(8,128)(2,1)} copy(bf16[16,8,2,128]{3,2,1,0:T(2,128)(2,1)} %bitcast.9) | data formatting | bytes 131072
  2.8 102.9 %layer.1 = (bf16[4,2,128,512]{3,2,1,0:T(8,128)(2,1)}, bf16[2,512,128]{2,1,0:T(8,128)(2,1)}) custom-call(s32[1]{0:T(128)S(6)} %copy.14.len_ref, bf16[128,4096]{1,0:T(8,128)(2,1)} %hidden_hbm.1, f32[1,4096]{1,0:T(1,128)} %bitcast.10, bf16[128,512]{1,0:T(8,128)(2,1)} %wq_ref.1, bf16[128,256]{1,0:T(8,128)(2,1)} %bitcast.8, ...), custom_call_target="tpu_custom_call" | custom-call | tf_op jit(solution)/shard_map/layer/pallas_call | solution.py:383
  105.6 3.0 %tail.1 = (bf16[4,2,128,512]{3,2,1,0:T(8,128)(2,1)}, f32[2,512,128]{2,1,0:T(8,128)}) custom-call(bf16[4,2,128,512]{3,2,1,0:T(8,128)(2,1)} %get-tuple-element.6.mixed_ref, bf16[2,512,128]{2,1,0:T(8,128)(2,1)} %get-tuple-element.7.sum_ref), custom_call_target="tpu_custom_call" | custom-call | tf_op jit(solution)/shard_map/tail/pallas_call | solution.py:429

commit v4 on v3

v4 whole, which is shorter than its diff:
```python
import functools
import math

import jax
import jax.numpy as jnp
import numpy as np
from jax import lax
from jax.experimental import pallas as pl
from jax.experimental.pallas import tpu as pltpu
from jax.sharding import PartitionSpec as P

HD = 128
MESH = pl.DeviceIdType.MESH
EPS = 1e-05
ROPE_BASE = 500000.0
F32 = jnp.float32
BF16 = jnp.bfloat16
NT = (((1,), (1,)), ((), ()))
CHIPS = 16
FAR_FIRST = sorted(range(1, CHIPS), key=lambda step: -min(step % 8, 8 - step % 8))
STEPS = (0, 1, -1, 2, -2, 3, -3, 4)
SLOT = {step: n for n, step in enumerate(STEPS)}
TICKS = ((0, 1), (1, 2), (3, 2), (5, 2), (7, 1))
X_PARTS = ((0, 3), (3, 2), (5, 3))
MAIN = 128

def layer_kernel(len_ref, hidden_hbm, gain_hbm, wq_ref, wkv_ref, cos_hbm, sin_hbm, cart_hbm, g_hbm,
                 mixed_ref, sum_ref,
                 hidden_ref, gain_ref, cos_ref, sin_ref, cart_ref, g_ref,
                 xn, wa, wb, acc_q, acc_kv, q_out, kv_out, q_in, kv_in, q_own, kv_own,
                 kx, vt, e_keep, d_keep, top_keep, grad, from_core, half, to_chips, from_chips, gathered, other,
                 local_sem, send_sem, recv_sem):
    dp, fsdp = lax.axis_index("dp"), lax.axis_index("fsdp")
    x, y_hi, y_lo, z, c = fsdp // 2, fsdp % 2, dp // 16, (dp // 2) % 8, dp % 2
    chip = dp // 2
    y = y_hi * 2 + y_lo
    turn = 1 - 2 * c
    length = len_ref[0]
    cart, seq = cart_ref.shape[1], 1024
    scale = HD ** -0.5
    factor = scale * math.log2(math.e)

    def at(dx=0, dy=0, dz=0, other=False):
        yy = lax.rem(y + dy + 8, 4)
        return (
            lax.rem(yy, 2) * 16 + lax.rem(z + dz + 16, 8) * 2 + (1 - c if other else c),
            lax.rem(x + dx + 8, 4) * 2 + yy // 2,
        )

    def peer(step):
        return lax.rem(chip + step, CHIPS)

    def ys(dy):
        yy = lax.rem(y + dy + 8, 4)
        return yy // 2, lax.rem(yy, 2)

    def xs(dx):
        return lax.rem(x + dx + 8, 4)

    slots, started = {}, []

    def send(name, ref, target, dst=None):
        assert name not in slots
        copy = pltpu.make_async_remote_copy(
            src_ref=ref, dst_ref=ref if dst is None else dst,
            send_sem=send_sem.at[len(started)], recv_sem=recv_sem.at[len(started)],
            device_id=target, device_id_type=MESH,
        )
        copy.start()
        slots[name] = copy
        started.append(copy)

    def arrived(name):
        slots[name].wait_recv()

    def main(dy, n, count=1):
        hi, lo = ys(dy)
        return wa.at[hi, lo, c, pl.ds(n, count)]

    def rest(dy, n):
        hi, lo = ys(dy)
        return wb.at[hi, lo, c, n]

    barrier = pltpu.get_barrier_semaphore()
    partners = [at(dx=1), at(dx=-1), at(dy=1), at(dy=-1), at(dy=2), at(dz=1), at(dz=-1), at(other=True)]
    peers = [(peer(step) * 2 + c, fsdp) for step in range(1, CHIPS)]
    for partner in partners + peers:
        pl.semaphore_signal(barrier, inc=1, device_id=partner, device_id_type=MESH)
    local = []
    for n, (ref, dst) in enumerate([
        (wkv_ref, rest(0, 0)),
        (wq_ref, wa.at[y_hi, y_lo, c, 0]),
        (hidden_hbm, hidden_ref), (gain_hbm, gain_ref),
        (cos_hbm.at[:, y_hi], cos_ref), (sin_hbm.at[:, y_hi], sin_ref), (cart_hbm, cart_ref), (g_hbm, g_ref),
    ]):
        copy = pltpu.make_async_copy(ref, dst, local_sem.at[n])
        copy.start()
        local.append(copy)
    pl.semaphore_wait(barrier, len(partners) + len(peers))
    for copy in local[:2]:
        copy.wait()

    def main_from_z(i):
        if i == 4:
            arrived(("za", 4, 1))
            arrived(("za", 4, -1))
        for way in (1, -1):
            if 0 < i < 4:
                arrived(("za", way * i))
            if i < 3:
                send(("za", way * (i + 1)), main(0, SLOT[way * i]), at(dz=-way), main(0, SLOT[way * (i + 1)]))
        if i == 3:
            for way, part in ((1, pl.ds(0, 64)), (-1, pl.ds(64, MAIN - 64))):
                send(("za", 4, way), main(0, SLOT[3 * way]).at[:, part], at(dz=-way), main(0, SLOT[4]).at[:, part])
        n, count = TICKS[i]
        for way in (1, -1):
            send(("ya", -way, i), main(0, n, count), at(dy=way))

    def main_from_y(i):
        n, count = TICKS[i]
        for way in (1, -1):
            arrived(("ya", way, i))
            if count == 2:
                ref = main(way, n + (1 - way) // 2)
            else:
                ref = main(way, n).at[:, pl.ds(0, 64) if way == 1 else pl.ds(64, MAIN - 64)]
            send(("ya", 2, way, i), ref, at(dy=-way))

    def main_to_core(i):
        n, count = TICKS[i]
        arrived(("ya", 2, 1, i))
        arrived(("ya", 2, -1, i))
        send(("ca", i), wa.at[:, :, c, pl.ds(n, count)], at(other=True))

    def rest_along_y():
        for way in (1, -1):
            send(("yb", -way), rest(0, 0), at(dy=way))

    def rest_further_along_y():
        for way in (1, -1):
            arrived(("yb", way))
            send(("yb", 2, way), rest(way, 0).at[pl.ds(0 if way == 1 else 64, 64)], at(dy=-way))

    def rest_from_z(i):
        if i == 0:
            arrived(("yb", 2, 1))
            arrived(("yb", 2, -1))
        for hi in range(2):
            if i == 4:
                arrived(("zb", 4, hi))
                continue
            for way in (1, -1):
                here = wb.at[hi, :, c, SLOT[way * i]]
                if i:
                    arrived(("zb", way * i, hi))
                if i < 3:
                    send(("zb", way * (i + 1), hi), here, at(dz=-way), wb.at[hi, :, c, SLOT[way * (i + 1)]])
                elif way == 1 - 2 * hi:
                    send(("zb", 4, hi), here, at(dz=-way), wb.at[hi, :, c, SLOT[4]])
        n, count = TICKS[i]
        send(("cb", i), wb.at[:, :, c, pl.ds(n, count)], at(other=True))

    def rows_out(part):
        n, count = X_PARTS[part]
        for way in (1, -1):
            send(("x", -way, part), xn.at[x, pl.ds(n, count)], at(dx=way))

    def rows_on(part):
        n, count = X_PARTS[part]
        for way in (1, -1):
            arrived(("x", way, part))
            send(("x", 2, way, part), xn.at[xs(way), pl.ds(n, count), (1 - way) // 2], at(dx=-way))

    def rows_ready(part):
        arrived(("x", 2, 1, part))
        arrived(("x", 2, -1, part))

    def multiply(n, hi):
        left = jnp.concatenate([xn[:, n, lo].reshape(512, 256) for lo in range(2)], axis=1)
        parts = [(lo, core) for lo in range(2) for core in range(2)]
        right = jnp.concatenate([wb[hi, lo, core, n] for lo, core in parts], axis=0)
        term = jnp.dot(left, right, preferred_element_type=F32)
        acc_kv[hi] = acc_kv[hi] + term if n else term
        right = jnp.concatenate([wa[hi, lo, core, n] for lo, core in parts], axis=0)
        term = jnp.dot(left, right, preferred_element_type=F32)
        acc_q[hi] = acc_q[hi] + term if n else term

    def ready(i):
        arrived(("ca", i))
        arrived(("cb", i))

    def multiply_all(i):
        ready(i)
        n, count = TICKS[i]
        for slot in range(n, n + count):
            for hi in range(2):
                multiply(slot, hi)

    rest_along_y()
    main_from_z(0)
    local[2].wait()
    local[3].wait()
    hidden = hidden_ref[...].astype(F32)
    inverse = lax.rsqrt(jnp.mean(hidden * hidden, axis=-1, keepdims=True) + EPS)
    for n, step in enumerate(STEPS):
        for lo in range(2):
            k = lo * 8 + lax.rem(z + step + 8, 8)
            cols = pl.ds(pl.multiple_of(k * 256, 256), 256)
            part = hidden_ref[:, cols].astype(F32) * inverse * gain_ref[:, cols]
            xn[x, n, lo] = part.astype(BF16)
    rows_out(0)
    rows_out(1)
    for copy in local[4:]:
        copy.wait()
    kx[:cart] = cart_ref[0]
    vt[:HD, :cart] = cart_ref[1].astype(F32).T.astype(BF16)
    spot = lax.broadcasted_iota(jnp.int32, (vt.shape[0] - HD, cart + seq), 1)
    vt[HD:] = jnp.where(spot < cart + length, 1.0, 0.0).astype(BF16)
    grad[...] = jnp.zeros_like(grad)
    rest_further_along_y()
    main_from_z(1)
    rest_from_z(0)
    main_from_y(0)
    main_from_z(2)
    rest_from_z(1)
    main_from_y(1)
    main_to_core(0)
    main_from_z(3)
    rows_on(0)
    rows_out(2)
    rest_from_z(2)
    main_from_y(2)
    main_to_core(1)
    main_from_z(4)
    rows_ready(0)
    multiply_all(0)
    rest_from_z(3)
    main_from_y(3)
    main_to_core(2)
    rows_on(1)
    multiply_all(1)
    main_from_y(4)
    main_to_core(3)
    rest_from_z(4)
    rows_on(2)
    rows_ready(1)
    multiply_all(2)
    main_to_core(4)
    rows_ready(2)
    multiply_all(3)
    ready(4)
    theirs = 1 - y_hi
    multiply(7, theirs)

    cos, sin = cos_ref[...].reshape(512, HD), sin_ref[...].reshape(512, HD)

    def turned(part):
        return (part * cos + pltpu.roll(part, HD // 2, 1) * sin).astype(BF16).reshape(4, HD, HD)

    def finish_kv(hi, out):
        out[0] = turned(acc_kv[hi, :, :HD])
        out[1] = acc_kv[hi, :, HD:].astype(BF16).reshape(4, HD, HD)

    first_kv = len(started)
    finish_kv(theirs, kv_out)
    send("kv", kv_out, at(dy=2), kv_in)
    first_q = len(started)
    for head in range(4):
        q_out[head] = turned(acc_q[theirs, :, head * HD:(head + 1) * HD])
        if head < 3:
            send(("q", head), q_out.at[head], at(dy=2), q_in.at[head])
    for j in (1, 0):
        blocks = pl.ds(2 * j, 2)
        send(("q", 3, j), q_out.at[3, blocks], at(dy=2), q_in.at[3, blocks])
    multiply(7, y_hi)
    for head in range(4):
        q_own[head] = turned(acc_q[y_hi, :, head * HD:(head + 1) * HD])

    def rows_of(hi):
        lane = lax.broadcasted_iota(jnp.int32, (1, 2 * HD), 1)
        return (lane // HD) * (2 * HD) + hi * HD + lax.rem(lane, HD)

    def grad_rows(head, j, hi):
        columns = pl.ds(pl.multiple_of(head * HD, HD), HD)
        g = g_ref[2 * j:2 * j + 2, hi, :, columns].reshape(2 * HD, HD)
        row = lax.broadcasted_iota(jnp.int32, (2 * HD, HD), 0)
        row = 4 * j * HD + (row // HD) * (2 * HD) + hi * HD + lax.rem(row, HD)
        return jnp.where(row < length, g, jnp.zeros_like(g))

    def cart_part(q, g):
        scores = lax.dot_general(kx[:cart], q, NT, preferred_element_type=F32)
        top = jnp.max(scores, axis=0, keepdims=True)
        d_prob = lax.dot_general(cart_ref[1], g, NT, preferred_element_type=F32)
        return jnp.exp2((scores - top) * factor), top, d_prob

    def attend(head, hi, js, qs, gs, carts):
        columns = pl.ds(pl.multiple_of(head * HD, HD), HD)
        near, far, outs = [], [], []
        for j, q in zip(js, qs):
            first = cart + 4 * j * HD
            near.append(lax.dot_general(kx[first:first + 4 * HD], q, NT, preferred_element_type=F32))
            far.append(lax.dot_general(kx[cart:first], q, NT, preferred_element_type=F32) if j else None)
        key = lax.broadcasted_iota(jnp.int32, (4 * HD, 2 * HD), 0)
        allowed = key <= rows_of(hi)
        for j, s_near, s_far, (e_cart, top_cart, _) in zip(js, near, far, carts):
            first = cart + 4 * j * HD
            s_near = jnp.where(allowed, s_near, -jnp.inf)
            top = jnp.maximum(top_cart, jnp.max(s_near, axis=0, keepdims=True))
            if j:
                top = jnp.maximum(top, jnp.max(s_far, axis=0, keepdims=True))
            shrink = jnp.exp2((top_cart - top) * factor)
            e_near = jnp.exp2((s_near - top) * factor).astype(BF16)
            out = jnp.dot(vt[:, :cart], e_cart.astype(BF16), preferred_element_type=F32) * shrink
            out += jnp.dot(vt[:, first:first + 4 * HD], e_near, preferred_element_type=F32)
            if j:
                e_far = jnp.exp2((s_far - top) * factor).astype(BF16)
                out += jnp.dot(vt[:, cart:first], e_far, preferred_element_type=F32)
            outs.append((out, shrink))
        probs, scores = [], []
        for j, g, (out, shrink), (e_cart, _, d_prob) in zip(js, gs, outs, carts):
            inverse = 1.0 / out[HD:HD + 1]
            out = out[:HD] * inverse
            mixed_ref[2 * j:2 * j + 2, hi, :, columns] = out.T.astype(BF16).reshape(2, HD, HD)
            delta = jnp.sum(out * g.astype(F32).T, axis=0, keepdims=True)
            prob = e_cart * (shrink * inverse)
            scores.append((prob * (d_prob - delta)).astype(BF16))
            probs.append(prob.astype(BF16))
        join = functools.partial(jnp.concatenate, axis=0)
        grad[1] += jnp.dot(jnp.concatenate(probs, axis=1), join(gs), preferred_element_type=F32)
        grad[0] += jnp.dot(jnp.concatenate(scores, axis=1), join(qs), preferred_element_type=F32)

    def pairs(q_ref, head, hi, js=(0, 1)):
        qs = [q_ref[head, 2 * j:2 * j + 2].reshape(2 * HD, HD) for j in js]
        return qs, [grad_rows(head, j, hi) for j in js]

    @pl.loop(0, 4)
    def _(head):
        qs, gs = pairs(q_own, head, y_hi)
        for j in range(2):
            e_cart, top, d_prob = cart_part(qs[j], gs[j])
            e_keep[head, j] = e_cart
            d_keep[head, j] = d_prob
            top_keep[head, j] = top

    finish_kv(y_hi, kv_own)
    for copy in started[:first_kv]:
        copy.wait_send()
    arrived("kv")
    for n in range(4):
        for hi, blocks in ((y_hi, kv_own), (theirs, kv_in)):
            first = pl.multiple_of((2 * n + hi) * HD, HD)
            live = first + lax.broadcasted_iota(jnp.int32, (HD, HD), 0) < length
            spare = jnp.broadcast_to(cart_ref[0, 0:1, :], (HD, HD))
            kx[pl.ds(cart + first, HD)] = jnp.where(live, blocks[0, n], spare)
            values = jnp.where(live, blocks[1, n].astype(F32), 0.0)
            vt[:HD, pl.ds(cart + first, HD)] = values.T.astype(BF16)

    @pl.loop(0, 4)
    def _(head):
        qs, gs = pairs(q_own, head, y_hi)
        kept = [(e_keep[head, j], top_keep[head, j], d_keep[head, j]) for j in range(2)]
        attend(head, y_hi, (0, 1), qs, gs, kept)

    @pl.loop(0, 3)
    def _(head):
        pltpu.make_async_remote_copy(
            src_ref=q_out.at[head], dst_ref=q_in.at[head], send_sem=send_sem.at[first_q + head],
            recv_sem=recv_sem.at[first_q + head], device_id=at(dy=2), device_id_type=MESH,
        ).wait_recv()
        qs, gs = pairs(q_in, head, theirs)
        attend(head, theirs, (0, 1), qs, gs, [cart_part(q, g) for q, g in zip(qs, gs)])

    for j in (1, 0):
        arrived(("q", 3, j))
        qs, gs = pairs(q_in, 3, theirs, (j,))
        attend(3, theirs, (j,), qs, gs, [cart_part(qs[0], gs[0])])

    rows = cart
    send("core_sum", grad.at[1 - c], at(other=True), from_core)
    arrived("core_sum")
    half[...] = (grad[c] + from_core[...]).reshape(half.shape)
    to_chips[...] = half[...].astype(BF16)
    for step in FAR_FIRST:
        send(("rs", step), to_chips.at[peer(step)], peers[step - 1], from_chips.at[step])
    done = len(started)
    for copy in started[first_kv:]:
        copy.wait_send()
    total = half[chip]
    for step in reversed(FAR_FIRST):
        arrived(("rs", step))
        total += from_chips[step].astype(F32)
    total = total * jnp.where(c == 0, scale, 1.0)
    gathered[chip] = total.astype(BF16)
    for step in FAR_FIRST:
        send(("ag", step), gathered.at[chip], peers[step - 1])
    for step in range(1, CHIPS):
        arrived(("ag", step))
    send("core_back", gathered, at(other=True), other)
    sum_ref[c] = gathered[...].reshape(rows, HD)
    arrived("core_back")
    sum_ref[1 - c] = other[...].reshape(rows, HD)
    for copy in started[done:]:
        copy.wait_send()


def rope_tables(cart, seq):
    frequency = np.power(np.float32(ROPE_BASE), np.arange(HD // 2, dtype=np.float32) * np.float32(-2.0 / HD))
    angles = (cart + np.arange(seq, dtype=np.float32))[:, None] * frequency.astype(np.float32)[None, :]
    cos, sin = np.cos(angles), np.sin(angles)
    shape = (seq // 256, 2, 128, HD)
    return (
        np.concatenate([cos, cos], axis=1).astype(np.float32).reshape(shape),
        np.concatenate([-sin, sin], axis=1).astype(np.float32).reshape(shape),
    )


def tail_kernel(mixed_ref, sum_ref, mixed_out, sum_out):
    mixed_out[...] = mixed_ref[...]
    sum_out[...] = sum_ref[...].astype(F32)


def on_device(hidden_in, lengths, cartridge, norm_gain, w_query, w_keyval, cotangent):
    cart = cartridge.shape[1]
    vmem, hbm = pl.BlockSpec(memory_space=pltpu.VMEM), pl.BlockSpec(memory_space=pltpu.HBM)
    cos, sin = rope_tables(cart, 1024)
    copies, share = 120, cart // CHIPS
    mixed, summed = pl.pallas_call(
        layer_kernel,
        name="layer",
        out_shape=(
            jax.ShapeDtypeStruct((4, 2, 128, 512), BF16),
            jax.ShapeDtypeStruct((2, cart, HD), BF16),
        ),
        in_specs=[pl.BlockSpec(memory_space=pltpu.SMEM)] + [hbm] * 8,
        out_specs=(vmem,) * 2,
        scratch_shapes=[
            pltpu.VMEM((128, 4096), BF16),
            pltpu.VMEM((1, 4096), F32),
            pltpu.VMEM((4, 128, HD), F32),
            pltpu.VMEM((4, 128, HD), F32),
            pltpu.VMEM((2, cart, HD), BF16),
            pltpu.VMEM((4, 2, 128, 512), BF16),
            pltpu.VMEM((4, 8, 2, 128, 256), BF16),
            pltpu.VMEM((2, 2, 2, 8, MAIN, 512), BF16),
            pltpu.VMEM((2, 2, 2, 8, 128, 256), BF16),
            pltpu.VMEM((2, 512, 512), F32),
            pltpu.VMEM((2, 512, 256), F32),
            pltpu.VMEM((4, 4, 128, HD), BF16),
            pltpu.VMEM((2, 4, 128, HD), BF16),
            pltpu.VMEM((4, 4, 128, HD), BF16),
            pltpu.VMEM((2, 4, 128, HD), BF16),
            pltpu.VMEM((4, 4, 128, HD), BF16),
            pltpu.VMEM((2, 4, 128, HD), BF16),
            pltpu.VMEM((cart + 1024, HD), BF16),
            pltpu.VMEM((HD + 16, cart + 1024), BF16),
            pltpu.VMEM((4, 2, cart, 256), F32),
            pltpu.VMEM((4, 2, cart, 256), F32),
            pltpu.VMEM((4, 2, 1, 256), F32),
            pltpu.VMEM((2, cart, HD), F32),
            pltpu.VMEM((cart, HD), F32),
            pltpu.VMEM((CHIPS, share, HD), F32),
            pltpu.VMEM((CHIPS, share, HD), BF16),
            pltpu.VMEM((CHIPS, share, HD), BF16),
            pltpu.VMEM((CHIPS, share, HD), BF16),
            pltpu.VMEM((CHIPS, share, HD), BF16),
            pltpu.SemaphoreType.DMA((8,)),
            pltpu.SemaphoreType.DMA((copies,)),
            pltpu.SemaphoreType.DMA((copies,)),
        ],
        compiler_params=pltpu.CompilerParams(collective_id=0, has_side_effects=True, vmem_limit_bytes=60 << 20),
    )(lengths, hidden_in, norm_gain.reshape(1, -1), w_query, w_keyval.reshape(128, 256), cos, sin, cartridge,
      cotangent.reshape(4, 2, 128, 512))
    blocks = (
        pl.BlockSpec((2, 2, 128, 512), lambda i: (i, 0, 0, 0)),
        pl.BlockSpec((1, cart, HD), lambda i: (i, 0, 0)),
    )
    mixed, summed = pl.pallas_call(
        tail_kernel,
        name="tail",
        out_shape=(
            jax.ShapeDtypeStruct(mixed.shape, BF16),
            jax.ShapeDtypeStruct(summed.shape, F32),
        ),
        grid=(2,),
        in_specs=blocks,
        out_specs=blocks,
    )(mixed, summed)
    return mixed.reshape(1024, 512), summed


def solution(mesh):
    in_specs = (
        P(("dp", "fsdp"), None),
        P("dp"),
        P(None, None, "fsdp"),
        P(),
        P("dp", "fsdp"),
        P("dp", None, "fsdp"),
        P("dp", "fsdp"),
    )
    out_specs = (P("dp", "fsdp"), P(None, None, "fsdp"))
    return jax.shard_map(on_device, mesh=mesh, in_specs=in_specs, out_specs=out_specs, check_vma=False)
```

time: 109 us -> 99.2 us (0.910)
  Pallas kernels: 106 us -> 96.2 us
    pallas_call x1, Pallas kernels: 103 us -> 94 us  [on_device(): pl.pallas_call(layer_kernel, name='layer', out_shape=(jax.ShapeDtypeStruc...]
where the time goes in v4:
time: 99.2 us; the launch traced here: 99 us
  Pallas kernels  96.2 us (97%)
  local copies, waits for them, and re-layouts  1.48 us (1%)
  between operations  1.29 us (1%)
    pallas_call x1, Pallas kernels, on_device(): pl.pallas_call(layer_kernel, name='layer', out_shape=(jax.ShapeDtypeStruc...  94 us
    pallas_call x1, Pallas kernels, on_device(): pl.pallas_call(tail_kernel, name='tail', out_shape=(jax.ShapeDtypeStruct(...  2.25 us

profile of v4, /device:TPU:1, one launch (start us, length us, event | category | flops | bytes accessed | tf_op | source)
XLA Modules:
  0.0 99.0 jit_solution(12573323450135377206)
XLA Ops:
  1.3 1.5 %copy.13 = bf16[16,8,2,128]{3,1,2,0:T(8,128)(2,1)} copy(bf16[16,8,2,128]{3,2,1,0:T(2,128)(2,1)} %bitcast.9) | data formatting | bytes 131072
  2.8 94.0 %layer.1 = (bf16[4,2,128,512]{3,2,1,0:T(8,128)(2,1)}, bf16[2,512,128]{2,1,0:T(8,128)(2,1)}) custom-call(s32[1]{0:T(128)S(6)} %copy.14.len_ref, bf16[128,4096]{1,0:T(8,128)(2,1)} %hidden_hbm.1, f32[1,4096]{1,0:T(1,128)} %bitcast.10, bf16[128,512]{1,0:T(8,128)(2,1)} %wq_ref.1, bf16[128,256]{1,0:T(8,128)(2,1)} %bitcast.8, ...), custom_call_target="tpu_custom_call" | custom-call | tf_op jit(solution)/shard_map/layer/pallas_call | solution.py:427
  96.7 2.3 %tail.1 = (bf16[4,2,128,512]{3,2,1,0:T(8,128)(2,1)}, f32[2,512,128]{2,1,0:T(8,128)}) custom-call(bf16[4,2,128,512]{3,2,1,0:T(8,128)(2,1)} %get-tuple-element.6.mixed_ref, bf16[2,512,128]{2,1,0:T(8,128)(2,1)} %get-tuple-element.7.sum_ref), custom_call_target="tpu_custom_call" | custom-call | tf_op jit(solution)/shard_map/tail/pallas_call | solution.py:477

commit v5 on v4

--- a/solution.py
+++ b/solution.py
@@ -28,8 +28,8 @@
                  mixed_ref, sum_ref,
                  hidden_ref, gain_ref, cos_ref, sin_ref, cart_ref, g_ref,
                  xn, wa, wb, acc_q, acc_kv, q_out, kv_out, q_in, kv_in, q_own, kv_own,
-                 kx, vt, e_keep, d_keep, top_keep, grad, from_core, half, to_chips, from_chips, gathered, other,
-                 local_sem, send_sem, recv_sem):
+                 k_new, vt_cart, vt_new, e_keep, d_keep, top_keep, out_keep, grad, from_core, half, to_chips, from_chips, gathered, other,
+                 kv_rows, kv_wide, local_sem, send_sem, recv_sem):
     dp, fsdp = lax.axis_index("dp"), lax.axis_index("fsdp")
     x, y_hi, y_lo, z, c = fsdp // 2, fsdp % 2, dp // 16, (dp // 2) % 8, dp % 2
     chip = dp // 2
@@ -88,7 +88,7 @@
         pl.semaphore_signal(barrier, inc=1, device_id=partner, device_id_type=MESH)
     local = []
     for n, (ref, dst) in enumerate([
-        (wkv_ref, rest(0, 0)),
+        (wkv_ref, kv_rows),
         (wq_ref, wa.at[y_hi, y_lo, c, 0]),
         (hidden_hbm, hidden_ref), (gain_hbm, gain_ref),
         (cos_hbm.at[:, y_hi], cos_ref), (sin_hbm.at[:, y_hi], sin_ref), (cart_hbm, cart_ref), (g_hbm, g_ref),
@@ -96,9 +96,11 @@
         copy = pltpu.make_async_copy(ref, dst, local_sem.at[n])
         copy.start()
         local.append(copy)
+    local[0].wait()
+    kv_wide[...] = kv_rows[...].astype(F32)
+    for i in range(2):
+        wb[y_hi, y_lo, c, 0, :, i * HD:(i + 1) * HD] = kv_wide[pl.ds(i, 128, 2)].astype(BF16)
     pl.semaphore_wait(barrier, len(partners) + len(peers))
-    for copy in local[:2]:
-        copy.wait()
 
     def main_from_z(i):
         if i == 4:
@@ -108,23 +110,29 @@
             if 0 < i < 4:
                 arrived(("za", way * i))
             if i < 3:
-                send(("za", way * (i + 1)), main(0, SLOT[way * i]), at(dz=-way), main(0, SLOT[way * (i + 1)]))
+                ref = main(0, SLOT[way * i]).at[0] if i else wq_ref
+                send(("za", way * (i + 1)), ref, at(dz=-way), main(0, SLOT[way * (i + 1)]).at[0])
         if i == 3:
             for way, part in ((1, pl.ds(0, 64)), (-1, pl.ds(64, MAIN - 64))):
                 send(("za", 4, way), main(0, SLOT[3 * way]).at[:, part], at(dz=-way), main(0, SLOT[4]).at[:, part])
         n, count = TICKS[i]
-        for way in (1, -1):
-            send(("ya", -way, i), main(0, n, count), at(dy=way))
+        for slot in range(n, n + count):
+            for way in (1, -1):
+                ref = main(0, slot).at[0]
+                send(("ya", -way, slot), ref if i else wq_ref, at(dy=way), ref)
 
     def main_from_y(i):
         n, count = TICKS[i]
         for way in (1, -1):
-            arrived(("ya", way, i))
-            if count == 2:
-                ref = main(way, n + (1 - way) // 2)
-            else:
-                ref = main(way, n).at[:, pl.ds(0, 64) if way == 1 else pl.ds(64, MAIN - 64)]
+            slot = n + (1 - way) // 2 if count == 2 else n
+            arrived(("ya", way, slot))
+            ref = main(way, slot)
+            if count == 1:
+                ref = ref.at[:, pl.ds(0, 64) if way == 1 else pl.ds(64, MAIN - 64)]
             send(("ya", 2, way, i), ref, at(dy=-way))
+        if count == 2:
+            arrived(("ya", 1, n + 1))
+            arrived(("ya", -1, n))
 
     def main_to_core(i):
         n, count = TICKS[i]
@@ -198,6 +206,7 @@
 
     rest_along_y()
     main_from_z(0)
+    local[1].wait()
     local[2].wait()
     local[3].wait()
     hidden = hidden_ref[...].astype(F32)
@@ -212,10 +221,8 @@
     rows_out(1)
     for copy in local[4:]:
         copy.wait()
-    kx[:cart] = cart_ref[0]
-    vt[:HD, :cart] = cart_ref[1].astype(F32).T.astype(BF16)
-    spot = lax.broadcasted_iota(jnp.int32, (vt.shape[0] - HD, cart + seq), 1)
-    vt[HD:] = jnp.where(spot < cart + length, 1.0, 0.0).astype(BF16)
+    vt_cart[:HD] = cart_ref[1].astype(F32).T.astype(BF16)
+    vt_cart[HD:] = jnp.ones((vt_cart.shape[0] - HD, cart), BF16)
     grad[...] = jnp.zeros_like(grad)
     rest_further_along_y()
     main_from_z(1)
@@ -276,9 +283,18 @@
     for head in range(4):
         q_own[head] = turned(acc_q[y_hi, :, head * HD:(head + 1) * HD])
 
-    def rows_of(hi):
-        lane = lax.broadcasted_iota(jnp.int32, (1, 2 * HD), 1)
-        return (lane // HD) * (2 * HD) + hi * HD + lax.rem(lane, HD)
+    def spots(hi, index):
+        return (index // HD) * (2 * HD) + hi * HD + lax.rem(index, HD)
+
+    def take_keys(hi, blocks):
+        spare = jnp.broadcast_to(cart_ref[0, 0:1, :], (HD, HD))
+        for n in range(4):
+            live = spots(hi, n * HD + lax.broadcasted_iota(jnp.int32, (HD, HD), 0)) < length
+            k_new[hi, n * HD:(n + 1) * HD] = jnp.where(live, blocks[0, n], spare)
+            values = jnp.where(live, blocks[1, n].astype(F32), 0.0)
+            vt_new[hi, :HD, n * HD:(n + 1) * HD] = values.T.astype(BF16)
+        live = spots(hi, lax.broadcasted_iota(jnp.int32, (vt_new.shape[1] - HD, 4 * HD), 1)) < length
+        vt_new[hi, HD:] = jnp.where(live, 1.0, 0.0).astype(BF16)
 
     def grad_rows(head, j, hi):
         columns = pl.ds(pl.multiple_of(head * HD, HD), HD)
@@ -287,37 +303,51 @@
         row = 4 * j * HD + (row // HD) * (2 * HD) + hi * HD + lax.rem(row, HD)
         return jnp.where(row < length, g, jnp.zeros_like(g))
 
-    def cart_part(q, g):
-        scores = lax.dot_general(kx[:cart], q, NT, preferred_element_type=F32)
-        top = jnp.max(scores, axis=0, keepdims=True)
-        d_prob = lax.dot_general(cart_ref[1], g, NT, preferred_element_type=F32)
-        return jnp.exp2((scores - top) * factor), top, d_prob
-
-    def attend(head, hi, js, qs, gs, carts):
+    def new_scores(key_hi, hi, j, q):
+        near = lax.dot_general(k_new[key_hi, 2 * j * HD:2 * (j + 1) * HD], q, NT, preferred_element_type=F32)
+        key = spots(key_hi, lax.broadcasted_iota(jnp.int32, near.shape, 0))
+        row = spots(hi, lax.broadcasted_iota(jnp.int32, (1, 2 * HD), 1))
+        near = jnp.where(key <= row, near, -jnp.inf)
+        if j == 0:
+            return [near]
+        return [lax.dot_general(k_new[key_hi, :2 * j * HD], q, NT, preferred_element_type=F32), near]
+
+    def highest(tops, scores):
+        for part in scores:
+            tops = jnp.maximum(tops, jnp.max(part, axis=0, keepdims=True))
+        return tops
+
+    def add_values(out, key_hi, scores, top):
+        first = 0
+        for part in scores:
+            last = first + part.shape[0]
+            weights = jnp.exp2((part - top) * factor).astype(BF16)
+            out += jnp.dot(vt_new[key_hi, :, first:last], weights, preferred_element_type=F32)
+            first = last
+        return out
+
+    def first_part(key_hi, hi, js, qs, gs):
+        carts = [lax.dot_general(cart_ref[0], q, NT, preferred_element_type=F32) for q in qs]
+        news = [new_scores(key_hi, hi, j, q) for j, q in zip(js, qs)]
+        d_probs = [lax.dot_general(cart_ref[1], g, NT, preferred_element_type=F32) for g in gs]
+        kept = []
+        for scores, new, d_prob in zip(carts, news, d_probs):
+            top = highest(jnp.max(scores, axis=0, keepdims=True), new)
+            e_cart = jnp.exp2((scores - top) * factor)
+            out = jnp.dot(vt_cart[...], e_cart.astype(BF16), preferred_element_type=F32)
+            kept.append((e_cart, top, d_prob, add_values(out, key_hi, new, top)))
+        return kept
+
+    def second_part(head, key_hi, hi, js, qs, gs, kept):
         columns = pl.ds(pl.multiple_of(head * HD, HD), HD)
-        near, far, outs = [], [], []
-        for j, q in zip(js, qs):
-            first = cart + 4 * j * HD
-            near.append(lax.dot_general(kx[first:first + 4 * HD], q, NT, preferred_element_type=F32))
-            far.append(lax.dot_general(kx[cart:first], q, NT, preferred_element_type=F32) if j else None)
-        key = lax.broadcasted_iota(jnp.int32, (4 * HD, 2 * HD), 0)
-        allowed = key <= rows_of(hi)
-        for j, s_near, s_far, (e_cart, top_cart, _) in zip(js, near, far, carts):
-            first = cart + 4 * j * HD
-            s_near = jnp.where(allowed, s_near, -jnp.inf)
-            top = jnp.maximum(top_cart, jnp.max(s_near, axis=0, keepdims=True))
-            if j:
-                top = jnp.maximum(top, jnp.max(s_far, axis=0, keepdims=True))
-            shrink = jnp.exp2((top_cart - top) * factor)
-            e_near = jnp.exp2((s_near - top) * factor).astype(BF16)
-            out = jnp.dot(vt[:, :cart], e_cart.astype(BF16), preferred_element_type=F32) * shrink
-            out += jnp.dot(vt[:, first:first + 4 * HD], e_near, preferred_element_type=F32)
-            if j:
-                e_far = jnp.exp2((s_far - top) * factor).astype(BF16)
-                out += jnp.dot(vt[:, cart:first], e_far, preferred_element_type=F32)
-            outs.append((out, shrink))
+        news = [new_scores(key_hi, hi, j, q) for j, q in zip(js, qs)]
+        outs = []
+        for new, (_, before, _, out) in zip(news, kept):
+            top = highest(before, new)
+            shrink = jnp.exp2((before - top) * factor)
+            outs.append((add_values(out * shrink, key_hi, new, top), shrink))
         probs, scores = [], []
-        for j, g, (out, shrink), (e_cart, _, d_prob) in zip(js, gs, outs, carts):
+        for j, g, (out, shrink), (e_cart, _, d_prob, _) in zip(js, gs, outs, kept):
             inverse = 1.0 / out[HD:HD + 1]
             out = out[:HD] * inverse
             mixed_ref[2 * j:2 * j + 2, hi, :, columns] = out.T.astype(BF16).reshape(2, HD, HD)
@@ -333,33 +363,24 @@
         qs = [q_ref[head, 2 * j:2 * j + 2].reshape(2 * HD, HD) for j in js]
         return qs, [grad_rows(head, j, hi) for j in js]
 
+    finish_kv(y_hi, kv_own)
+    take_keys(y_hi, kv_own)
+    both = (0, 1)
+
     @pl.loop(0, 4)
     def _(head):
-        qs, gs = pairs(q_own, head, y_hi)
-        for j in range(2):
-            e_cart, top, d_prob = cart_part(qs[j], gs[j])
-            e_keep[head, j] = e_cart
-            d_keep[head, j] = d_prob
-            top_keep[head, j] = top
-
-    finish_kv(y_hi, kv_own)
+        for j, kept in enumerate(first_part(y_hi, y_hi, both, *pairs(q_own, head, y_hi))):
+            e_keep[head, j], top_keep[head, j], d_keep[head, j], out_keep[head, j] = kept
+
     for copy in started[:first_kv]:
         copy.wait_send()
     arrived("kv")
-    for n in range(4):
-        for hi, blocks in ((y_hi, kv_own), (theirs, kv_in)):
-            first = pl.multiple_of((2 * n + hi) * HD, HD)
-            live = first + lax.broadcasted_iota(jnp.int32, (HD, HD), 0) < length
-            spare = jnp.broadcast_to(cart_ref[0, 0:1, :], (HD, HD))
-            kx[pl.ds(cart + first, HD)] = jnp.where(live, blocks[0, n], spare)
-            values = jnp.where(live, blocks[1, n].astype(F32), 0.0)
-            vt[:HD, pl.ds(cart + first, HD)] = values.T.astype(BF16)
+    take_keys(theirs, kv_in)
 
     @pl.loop(0, 4)
     def _(head):
-        qs, gs = pairs(q_own, head, y_hi)
-        kept = [(e_keep[head, j], top_keep[head, j], d_keep[head, j]) for j in range(2)]
-        attend(head, y_hi, (0, 1), qs, gs, kept)
+        kept = [(e_keep[head, j], top_keep[head, j], d_keep[head, j], out_keep[head, j]) for j in both]
+        second_part(head, theirs, y_hi, both, *pairs(q_own, head, y_hi), kept)
 
     @pl.loop(0, 3)
     def _(head):
@@ -368,12 +389,12 @@
             recv_sem=recv_sem.at[first_q + head], device_id=at(dy=2), device_id_type=MESH,
         ).wait_recv()
         qs, gs = pairs(q_in, head, theirs)
-        attend(head, theirs, (0, 1), qs, gs, [cart_part(q, g) for q, g in zip(qs, gs)])
+        second_part(head, theirs, theirs, both, qs, gs, first_part(y_hi, theirs, both, qs, gs))
 
     for j in (1, 0):
         arrived(("q", 3, j))
         qs, gs = pairs(q_in, 3, theirs, (j,))
-        attend(3, theirs, (j,), qs, gs, [cart_part(qs[0], gs[0])])
+        second_part(3, theirs, theirs, (j,), qs, gs, first_part(y_hi, theirs, (j,), qs, gs))
 
     rows = cart
     send("core_sum", grad.at[1 - c], at(other=True), from_core)
@@ -451,11 +472,13 @@
             pltpu.VMEM((2, 4, 128, HD), BF16),
             pltpu.VMEM((4, 4, 128, HD), BF16),
             pltpu.VMEM((2, 4, 128, HD), BF16),
-            pltpu.VMEM((cart + 1024, HD), BF16),
-            pltpu.VMEM((HD + 16, cart + 1024), BF16),
+            pltpu.VMEM((2, 512, HD), BF16),
+            pltpu.VMEM((HD + 16, cart), BF16),
+            pltpu.VMEM((2, HD + 16, 512), BF16),
             pltpu.VMEM((4, 2, cart, 256), F32),
             pltpu.VMEM((4, 2, cart, 256), F32),
             pltpu.VMEM((4, 2, 1, 256), F32),
+            pltpu.VMEM((4, 2, HD + 16, 256), F32),
             pltpu.VMEM((2, cart, HD), F32),
             pltpu.VMEM((cart, HD), F32),
             pltpu.VMEM((CHIPS, share, HD), F32),
@@ -463,12 +486,14 @@
             pltpu.VMEM((CHIPS, share, HD), BF16),
             pltpu.VMEM((CHIPS, share, HD), BF16),
             pltpu.VMEM((CHIPS, share, HD), BF16),
+            pltpu.VMEM((256, HD), BF16),
+            pltpu.VMEM((256, HD), F32),
             pltpu.SemaphoreType.DMA((8,)),
             pltpu.SemaphoreType.DMA((copies,)),
             pltpu.SemaphoreType.DMA((copies,)),
         ],
         compiler_params=pltpu.CompilerParams(collective_id=0, has_side_effects=True, vmem_limit_bytes=60 << 20),
-    )(lengths, hidden_in, norm_gain.reshape(1, -1), w_query, w_keyval.reshape(128, 256), cos, sin, cartridge,
+    )(lengths, hidden_in, norm_gain.reshape(1, -1), w_query, w_keyval.reshape(256, HD), cos, sin, cartridge,
       cotangent.reshape(4, 2, 128, 512))
     blocks = (
         pl.BlockSpec((2, 2, 128, 512), lambda i: (i, 0, 0, 0)),

time: 99.2 us -> 96.5 us (0.973)
  local copies, waits for them, and re-layouts: 1.48 us -> 0 us
  Pallas kernels: 96.2 us -> 95.1 us
    unnamed x1 -> x0, local copies, waits for them, and re-layouts: 1.48 us -> none
    pallas_call x1, Pallas kernels: 94 us -> 92.8 us  [on_device(): pl.pallas_call(layer_kernel, name='layer', out_shape=(jax.ShapeDtypeStruc...]
where the time goes in v5:
time: 96.5 us; the launch traced here: 96.4 us
  Pallas kernels  95.1 us (99%)
  between operations  1.29 us (1%)
    pallas_call x1, Pallas kernels, on_device(): pl.pallas_call(layer_kernel, name='layer', out_shape=(jax.ShapeDtypeStruc...  92.8 us
    pallas_call x1, Pallas kernels, on_device(): pl.pallas_call(tail_kernel, name='tail', out_shape=(jax.ShapeDtypeStruct(...  2.25 us

profile of v5, /device:TPU:1, one launch (start us, length us, event | category | flops | bytes accessed | tf_op | source)
XLA Modules:
  0.0 96.4 jit_solution(15669022603855254390)
XLA Ops:
  1.3 92.8 %layer.1 = (bf16[4,2,128,512]{3,2,1,0:T(8,128)(2,1)}, bf16[2,512,128]{2,1,0:T(8,128)(2,1)}) custom-call(s32[1]{0:T(128)S(6)} %copy.11.len_ref, bf16[128,4096]{1,0:T(8,128)(2,1)} %hidden_hbm.1, f32[1,4096]{1,0:T(1,128)} %bitcast.6, bf16[128,512]{1,0:T(8,128)(2,1)} %wq_ref.1, bf16[256,128]{1,0:T(8,128)(2,1)} %bitcast.5, ...), custom_call_target="tpu_custom_call" | custom-call | tf_op jit(solution)/shard_map/layer/pallas_call | solution.py:448
  94.1 2.3 %tail.1 = (bf16[4,2,128,512]{3,2,1,0:T(8,128)(2,1)}, f32[2,512,128]{2,1,0:T(8,128)}) custom-call(bf16[4,2,128,512]{3,2,1,0:T(8,128)(2,1)} %get-tuple-element.6.mixed_ref, bf16[2,512,128]{2,1,0:T(8,128)(2,1)} %get-tuple-element.7.sum_ref), custom_call_target="tpu_custom_call" | custom-call | tf_op jit(solution)/shard_map/tail/pallas_call | solution.py:502

commit v6 on v5

--- a/solution.py
+++ b/solution.py
@@ -183,26 +183,27 @@
         arrived(("x", 2, 1, part))
         arrived(("x", 2, -1, part))
 
-    def multiply(n, hi):
+    def operands(weights, n, hi):
         left = jnp.concatenate([xn[:, n, lo].reshape(512, 256) for lo in range(2)], axis=1)
-        parts = [(lo, core) for lo in range(2) for core in range(2)]
-        right = jnp.concatenate([wb[hi, lo, core, n] for lo, core in parts], axis=0)
-        term = jnp.dot(left, right, preferred_element_type=F32)
+        right = [weights[hi, lo, core, n] for lo in range(2) for core in range(2)]
+        return left, jnp.concatenate(right, axis=0)
+
+    def multiply_kv(n, hi):
+        term = jnp.dot(*operands(wb, n, hi), preferred_element_type=F32)
         acc_kv[hi] = acc_kv[hi] + term if n else term
-        right = jnp.concatenate([wa[hi, lo, core, n] for lo, core in parts], axis=0)
-        term = jnp.dot(left, right, preferred_element_type=F32)
+
+    def multiply_q(n, hi):
+        term = jnp.dot(*operands(wa, n, hi), preferred_element_type=F32)
         acc_q[hi] = acc_q[hi] + term if n else term
 
-    def ready(i):
+    def multiply_all(i):
         arrived(("ca", i))
         arrived(("cb", i))
-
-    def multiply_all(i):
-        ready(i)
         n, count = TICKS[i]
         for slot in range(n, n + count):
             for hi in range(2):
-                multiply(slot, hi)
+                multiply_kv(slot, hi)
+                multiply_q(slot, hi)
 
     rest_along_y()
     main_from_z(0)
@@ -252,12 +253,7 @@
     rows_on(2)
     rows_ready(1)
     multiply_all(2)
-    main_to_core(4)
-    rows_ready(2)
-    multiply_all(3)
-    ready(4)
     theirs = 1 - y_hi
-    multiply(7, theirs)
 
     cos, sin = cos_ref[...].reshape(512, HD), sin_ref[...].reshape(512, HD)
 
@@ -267,21 +263,6 @@
     def finish_kv(hi, out):
         out[0] = turned(acc_kv[hi, :, :HD])
         out[1] = acc_kv[hi, :, HD:].astype(BF16).reshape(4, HD, HD)
-
-    first_kv = len(started)
-    finish_kv(theirs, kv_out)
-    send("kv", kv_out, at(dy=2), kv_in)
-    first_q = len(started)
-    for head in range(4):
-        q_out[head] = turned(acc_q[theirs, :, head * HD:(head + 1) * HD])
-        if head < 3:
-            send(("q", head), q_out.at[head], at(dy=2), q_in.at[head])
-    for j in (1, 0):
-        blocks = pl.ds(2 * j, 2)
-        send(("q", 3, j), q_out.at[3, blocks], at(dy=2), q_in.at[3, blocks])
-    multiply(7, y_hi)
-    for head in range(4):
-        q_own[head] = turned(acc_q[y_hi, :, head * HD:(head + 1) * HD])
 
     def spots(hi, index):
         return (index // HD) * (2 * HD) + hi * HD + lax.rem(index, HD)
@@ -295,6 +276,37 @@
             vt_new[hi, :HD, n * HD:(n + 1) * HD] = values.T.astype(BF16)
         live = spots(hi, lax.broadcasted_iota(jnp.int32, (vt_new.shape[1] - HD, 4 * HD), 1)) < length
         vt_new[hi, HD:] = jnp.where(live, 1.0, 0.0).astype(BF16)
+
+    rows_ready(2)
+    arrived(("cb", 3))
+    arrived(("cb", 4))
+    for n in (5, 6, 7):
+        multiply_kv(n, theirs)
+    first_kv = len(started)
+    finish_kv(theirs, kv_out)
+    send("kv", kv_out, at(dy=2), kv_in)
+    main_to_core(4)
+    for n in (5, 6, 7):
+        multiply_kv(n, y_hi)
+    finish_kv(y_hi, kv_own)
+    take_keys(y_hi, kv_own)
+    arrived(("ca", 3))
+    for n in (5, 6):
+        for hi in (0, 1):
+            multiply_q(n, hi)
+    arrived(("ca", 4))
+    multiply_q(7, theirs)
+    first_q = len(started)
+    for head in range(4):
+        q_out[head] = turned(acc_q[theirs, :, head * HD:(head + 1) * HD])
+        if head < 3:
+            send(("q", head), q_out.at[head], at(dy=2), q_in.at[head])
+    for j in (1, 0):
+        blocks = pl.ds(2 * j, 2)
+        send(("q", 3, j), q_out.at[3, blocks], at(dy=2), q_in.at[3, blocks])
+    multiply_q(7, y_hi)
+    for head in range(4):
+        q_own[head] = turned(acc_q[y_hi, :, head * HD:(head + 1) * HD])
 
     def grad_rows(head, j, hi):
         columns = pl.ds(pl.multiple_of(head * HD, HD), HD)
@@ -363,8 +375,6 @@
         qs = [q_ref[head, 2 * j:2 * j + 2].reshape(2 * HD, HD) for j in js]
         return qs, [grad_rows(head, j, hi) for j in js]
 
-    finish_kv(y_hi, kv_own)
-    take_keys(y_hi, kv_own)
     both = (0, 1)
 
     @pl.loop(0, 4)

time: 96.5 us -> 95.8 us (level)
  no operation moved by 1% of the time
where the time goes in v6:
time: 95.8 us; the launch traced here: 95.7 us
  Pallas kernels  94.4 us (99%)
  between operations  1.29 us (1%)
    pallas_call x1, Pallas kernels, on_device(): pl.pallas_call(layer_kernel, name='layer', out_shape=(jax.ShapeDtypeStruc...  92.1 us
    pallas_call x1, Pallas kernels, on_device(): pl.pallas_call(tail_kernel, name='tail', out_shape=(jax.ShapeDtypeStruct(...  2.25 us

profile of v6, /device:TPU:1, one launch (start us, length us, event | category | flops | bytes accessed | tf_op | source)
XLA Modules:
  0.0 95.7 jit_solution(12279112967035830518)
XLA Ops:
  1.3 92.1 %layer.1 = (bf16[4,2,128,512]{3,2,1,0:T(8,128)(2,1)}, bf16[2,512,128]{2,1,0:T(8,128)(2,1)}) custom-call(s32[1]{0:T(128)S(6)} %copy.11.len_ref, bf16[128,4096]{1,0:T(8,128)(2,1)} %hidden_hbm.1, f32[1,4096]{1,0:T(1,128)} %bitcast.6, bf16[128,512]{1,0:T(8,128)(2,1)} %wq_ref.1, bf16[256,128]{1,0:T(8,128)(2,1)} %bitcast.5, ...), custom_call_target="tpu_custom_call" | custom-call | tf_op jit(solution)/shard_map/layer/pallas_call | solution.py:458
  93.4 2.3 %tail.1 = (bf16[4,2,128,512]{3,2,1,0:T(8,128)(2,1)}, f32[2,512,128]{2,1,0:T(8,128)}) custom-call(bf16[4,2,128,512]{3,2,1,0:T(8,128)(2,1)} %get-tuple-element.6.mixed_ref, bf16[2,512,128]{2,1,0:T(8,128)(2,1)} %get-tuple-element.7.sum_ref), custom_call_target="tpu_custom_call" | custom-call | tf_op jit(solution)/shard_map/tail/pallas_call | solution.py:512

commit v7 on v6

--- a/solution.py
+++ b/solution.py
@@ -28,7 +28,7 @@
                  mixed_ref, sum_ref,
                  hidden_ref, gain_ref, cos_ref, sin_ref, cart_ref, g_ref,
                  xn, wa, wb, acc_q, acc_kv, q_out, kv_out, q_in, kv_in, q_own, kv_own,
-                 k_new, vt_cart, vt_new, e_keep, d_keep, top_keep, out_keep, grad, from_core, half, to_chips, from_chips, gathered, other,
+                 k_new, vt_cart, vt_new, e_keep, d_keep, g_turned, top_keep, out_keep, grad, from_core, half, to_chips, from_chips, gathered, other,
                  kv_rows, kv_wide, local_sem, send_sem, recv_sem):
     dp, fsdp = lax.axis_index("dp"), lax.axis_index("fsdp")
     x, y_hi, y_lo, z, c = fsdp // 2, fsdp % 2, dp // 16, (dp // 2) % 8, dp % 2
@@ -225,6 +225,22 @@
     vt_cart[:HD] = cart_ref[1].astype(F32).T.astype(BF16)
     vt_cart[HD:] = jnp.ones((vt_cart.shape[0] - HD, cart), BF16)
     grad[...] = jnp.zeros_like(grad)
+    def grad_rows(head, j, hi):
+        columns = pl.ds(pl.multiple_of(head * HD, HD), HD)
+        g = g_ref[2 * j:2 * j + 2, hi, :, columns].reshape(2 * HD, HD)
+        row = lax.broadcasted_iota(jnp.int32, (2 * HD, HD), 0)
+        row = 4 * j * HD + (row // HD) * (2 * HD) + hi * HD + lax.rem(row, HD)
+        return jnp.where(row < length, g, jnp.zeros_like(g))
+
+    def value_products(hi):
+        @pl.loop(0, 4)
+        def _(head):
+            for j in range(2):
+                g = grad_rows(head, j, hi)
+                d_keep[hi, head, j] = lax.dot_general(cart_ref[1], g, NT, preferred_element_type=F32)
+                g_turned[hi, head, j] = g.astype(F32).T
+
+    value_products(y_hi)
     rest_further_along_y()
     main_from_z(1)
     rest_from_z(0)
@@ -240,6 +256,7 @@
     main_from_y(2)
     main_to_core(1)
     main_from_z(4)
+    value_products(1 - y_hi)
     rows_ready(0)
     multiply_all(0)
     rest_from_z(3)
@@ -308,13 +325,6 @@
     for head in range(4):
         q_own[head] = turned(acc_q[y_hi, :, head * HD:(head + 1) * HD])
 
-    def grad_rows(head, j, hi):
-        columns = pl.ds(pl.multiple_of(head * HD, HD), HD)
-        g = g_ref[2 * j:2 * j + 2, hi, :, columns].reshape(2 * HD, HD)
-        row = lax.broadcasted_iota(jnp.int32, (2 * HD, HD), 0)
-        row = 4 * j * HD + (row // HD) * (2 * HD) + hi * HD + lax.rem(row, HD)
-        return jnp.where(row < length, g, jnp.zeros_like(g))
-
     def new_scores(key_hi, hi, j, q):
         near = lax.dot_general(k_new[key_hi, 2 * j * HD:2 * (j + 1) * HD], q, NT, preferred_element_type=F32)
         key = spots(key_hi, lax.broadcasted_iota(jnp.int32, near.shape, 0))
@@ -338,34 +348,33 @@
             first = last
         return out
 
-    def first_part(key_hi, hi, js, qs, gs):
+    def first_part(key_hi, hi, js, qs):
         carts = [lax.dot_general(cart_ref[0], q, NT, preferred_element_type=F32) for q in qs]
         news = [new_scores(key_hi, hi, j, q) for j, q in zip(js, qs)]
-        d_probs = [lax.dot_general(cart_ref[1], g, NT, preferred_element_type=F32) for g in gs]
         kept = []
-        for scores, new, d_prob in zip(carts, news, d_probs):
+        for scores, new in zip(carts, news):
             top = highest(jnp.max(scores, axis=0, keepdims=True), new)
             e_cart = jnp.exp2((scores - top) * factor)
             out = jnp.dot(vt_cart[...], e_cart.astype(BF16), preferred_element_type=F32)
-            kept.append((e_cart, top, d_prob, add_values(out, key_hi, new, top)))
+            kept.append((e_cart, top, add_values(out, key_hi, new, top)))
         return kept
 
     def second_part(head, key_hi, hi, js, qs, gs, kept):
         columns = pl.ds(pl.multiple_of(head * HD, HD), HD)
         news = [new_scores(key_hi, hi, j, q) for j, q in zip(js, qs)]
         outs = []
-        for new, (_, before, _, out) in zip(news, kept):
+        for new, (_, before, out) in zip(news, kept):
             top = highest(before, new)
             shrink = jnp.exp2((before - top) * factor)
             outs.append((add_values(out * shrink, key_hi, new, top), shrink))
         probs, scores = [], []
-        for j, g, (out, shrink), (e_cart, _, d_prob, _) in zip(js, gs, outs, kept):
+        for j, (out, shrink), (e_cart, _, _) in zip(js, outs, kept):
             inverse = 1.0 / out[HD:HD + 1]
             out = out[:HD] * inverse
             mixed_ref[2 * j:2 * j + 2, hi, :, columns] = out.T.astype(BF16).reshape(2, HD, HD)
-            delta = jnp.sum(out * g.astype(F32).T, axis=0, keepdims=True)
+            delta = jnp.sum(out * g_turned[hi, head, j], axis=0, keepdims=True)
             prob = e_cart * (shrink * inverse)
-            scores.append((prob * (d_prob - delta)).astype(BF16))
+            scores.append((prob * (d_keep[hi, head, j] - delta)).astype(BF16))
             probs.append(prob.astype(BF16))
         join = functools.partial(jnp.concatenate, axis=0)
         grad[1] += jnp.dot(jnp.concatenate(probs, axis=1), join(gs), preferred_element_type=F32)
@@ -379,8 +388,9 @@
 
     @pl.loop(0, 4)
     def _(head):
-        for j, kept in enumerate(first_part(y_hi, y_hi, both, *pairs(q_own, head, y_hi))):
-            e_keep[head, j], top_keep[head, j], d_keep[head, j], out_keep[head, j] = kept
+        qs, _ = pairs(q_own, head, y_hi)
+        for j, kept in enumerate(first_part(y_hi, y_hi, both, qs)):
+            e_keep[head, j], top_keep[head, j], out_keep[head, j] = kept
 
     for copy in started[:first_kv]:
         copy.wait_send()
@@ -389,7 +399,7 @@
 
     @pl.loop(0, 4)
     def _(head):
-        kept = [(e_keep[head, j], top_keep[head, j], d_keep[head, j], out_keep[head, j]) for j in both]
+        kept = [(e_keep[head, j], top_keep[head, j], out_keep[head, j]) for j in both]
         second_part(head, theirs, y_hi, both, *pairs(q_own, head, y_hi), kept)
 
     @pl.loop(0, 3)
@@ -399,12 +409,12 @@
             recv_sem=recv_sem.at[first_q + head], device_id=at(dy=2), device_id_type=MESH,
         ).wait_recv()
         qs, gs = pairs(q_in, head, theirs)
-        second_part(head, theirs, theirs, both, qs, gs, first_part(y_hi, theirs, both, qs, gs))
+        second_part(head, theirs, theirs, both, qs, gs, first_part(y_hi, theirs, both, qs))
 
     for j in (1, 0):
         arrived(("q", 3, j))
         qs, gs = pairs(q_in, 3, theirs, (j,))
-        second_part(3, theirs, theirs, (j,), qs, gs, first_part(y_hi, theirs, (j,), qs, gs))
+        second_part(3, theirs, theirs, (j,), qs, gs, first_part(y_hi, theirs, (j,), qs))
 
     rows = cart
     send("core_sum", grad.at[1 - c], at(other=True), from_core)
@@ -486,7 +496,8 @@
             pltpu.VMEM((HD + 16, cart), BF16),
             pltpu.VMEM((2, HD + 16, 512), BF16),
             pltpu.VMEM((4, 2, cart, 256), F32),
-            pltpu.VMEM((4, 2, cart, 256), F32),
+            pltpu.VMEM((2, 4, 2, cart, 256), F32),
+            pltpu.VMEM((2, 4, 2, HD, 256), F32),
             pltpu.VMEM((4, 2, 1, 256), F32),
             pltpu.VMEM((4, 2, HD + 16, 256), F32),
             pltpu.VMEM((2, cart, HD), F32),

time: 95.8 us -> 94.5 us (0.986)
  Pallas kernels: 94.4 us -> 93.1 us
    pallas_call x1, Pallas kernels: 92.1 us -> 90.8 us  [on_device(): pl.pallas_call(layer_kernel, name='layer', out_shape=(jax.ShapeDtypeStruc...]
where the time goes in v7:
time: 94.5 us; the launch traced here: 94.4 us
  Pallas kernels  93.1 us (99%)
  between operations  1.29 us (1%)
    pallas_call x1, Pallas kernels, on_device(): pl.pallas_call(layer_kernel, name='layer', out_shape=(jax.ShapeDtypeStruc...  90.8 us
    pallas_call x1, Pallas kernels, on_device(): pl.pallas_call(tail_kernel, name='tail', out_shape=(jax.ShapeDtypeStruct(...  2.25 us

profile of v7, /device:TPU:1, one launch (start us, length us, event | category | flops | bytes accessed | tf_op | source)
XLA Modules:
  0.0 94.4 jit_solution(17172468637615236247)
XLA Ops:
  1.3 90.8 %layer.1 = (bf16[4,2,128,512]{3,2,1,0:T(8,128)(2,1)}, bf16[2,512,128]{2,1,0:T(8,128)(2,1)}) custom-call(s32[1]{0:T(128)S(6)} %copy.11.len_ref, bf16[128,4096]{1,0:T(8,128)(2,1)} %hidden_hbm.1, f32[1,4096]{1,0:T(1,128)} %bitcast.6, bf16[128,512]{1,0:T(8,128)(2,1)} %wq_ref.1, bf16[256,128]{1,0:T(8,128)(2,1)} %bitcast.5, ...), custom_call_target="tpu_custom_call" | custom-call | tf_op jit(solution)/shard_map/layer/pallas_call | solution.py:468
  92.1 2.3 %tail.1 = (bf16[4,2,128,512]{3,2,1,0:T(8,128)(2,1)}, f32[2,512,128]{2,1,0:T(8,128)}) custom-call(bf16[4,2,128,512]{3,2,1,0:T(8,128)(2,1)} %get-tuple-element.6.mixed_ref, bf16[2,512,128]{2,1,0:T(8,128)(2,1)} %get-tuple-element.7.sum_ref), custom_call_target="tpu_custom_call" | custom-call | tf_op jit(solution)/shard_map/tail/pallas_call | solution.py:523

commit v8 on v7

--- a/solution.py
+++ b/solution.py
@@ -517,8 +517,8 @@
     )(lengths, hidden_in, norm_gain.reshape(1, -1), w_query, w_keyval.reshape(256, HD), cos, sin, cartridge,
       cotangent.reshape(4, 2, 128, 512))
     blocks = (
-        pl.BlockSpec((2, 2, 128, 512), lambda i: (i, 0, 0, 0)),
-        pl.BlockSpec((1, cart, HD), lambda i: (i, 0, 0)),
+        pl.BlockSpec((1, 2, 128, 512), lambda i: (i, 0, 0, 0)),
+        pl.BlockSpec((1, cart // 2, HD), lambda i: (i // 2, i % 2, 0)),
     )
     mixed, summed = pl.pallas_call(
         tail_kernel,
@@ -527,7 +527,7 @@
             jax.ShapeDtypeStruct(mixed.shape, BF16),
             jax.ShapeDtypeStruct(summed.shape, F32),
         ),
-        grid=(2,),
+        grid=(4,),
         in_specs=blocks,
         out_specs=blocks,
     )(mixed, summed)

time: 94.5 us -> 95.8 us (1.014)
  Pallas kernels: 93.1 us -> 94.3 us
    pallas_call x1, Pallas kernels: 2.25 us -> 3.47 us  [on_device(): pl.pallas_call(tail_kernel, name='tail', out_shape=(jax.ShapeDtypeStruct(...]
where the time goes in v8:
time: 95.8 us; the launch traced here: 95.6 us
  Pallas kernels  94.3 us (98%)
  between operations  1.29 us (1%)
    pallas_call x1, Pallas kernels, on_device(): pl.pallas_call(layer_kernel, name='layer', out_shape=(jax.ShapeDtypeStruc...  90.8 us
    pallas_call x1, Pallas kernels, on_device(): pl.pallas_call(tail_kernel, name='tail', out_shape=(jax.ShapeDtypeStruct(...  3.47 us

profile of v8, /device:TPU:1, one launch (start us, length us, event | category | flops | bytes accessed | tf_op | source)
XLA Modules:
  0.0 95.6 jit_solution(12930410636621734017)
XLA Ops:
  1.3 90.8 %layer.1 = (bf16[4,2,128,512]{3,2,1,0:T(8,128)(2,1)}, bf16[2,512,128]{2,1,0:T(8,128)(2,1)}) custom-call(s32[1]{0:T(128)S(6)} %copy.11.len_ref, bf16[128,4096]{1,0:T(8,128)(2,1)} %hidden_hbm.1, f32[1,4096]{1,0:T(1,128)} %bitcast.6, bf16[128,512]{1,0:T(8,128)(2,1)} %wq_ref.1, bf16[256,128]{1,0:T(8,128)(2,1)} %bitcast.5, ...), custom_call_target="tpu_custom_call" | custom-call | tf_op jit(solution)/shard_map/layer/pallas_call | solution.py:468
  92.1 3.5 %tail.1 = (bf16[4,2,128,512]{3,2,1,0:T(8,128)(2,1)}, f32[2,512,128]{2,1,0:T(8,128)}) custom-call(bf16[4,2,128,512]{3,2,1,0:T(8,128)(2,1)} %get-tuple-element.6.mixed_ref, bf16[2,512,128]{2,1,0:T(8,128)(2,1)} %get-tuple-element.7.sum_ref), custom_call_target="tpu_custom_call" | custom-call | tf_op jit(solution)/shard_map/tail/pallas_call | solution.py:523
